TPU v7x, 512 devices: a whole 4x4x16 slice. The times are simulated.
512 devices in a mesh: dp: 64 (over x, z), cent: 8 (over y, core).
Axes of the slice: x: 4, y: 4, z: 16, core: 2. Of those that a mesh axis runs over, the one named last changes fastest.
Arguments:
- points: bfloat16 [65536, 768], P('dp'), may hold values from -60 to 60
- centroids: bfloat16 [8192, 768], P('cent'), may hold values from -60 to 60
Outputs:
- new_centroids: bfloat16 [8192, 768], P('cent')
All inputs are finite; a program needn't handle non-finite values.
Results may differ from a plain program's by a relative error of at most 0.0022.
Values may be sent and summed in bfloat16 or wider, within the bound.
A program may use at most 64 MiB of HBM per device.

v0:
```python
import math

import jax
import jax.numpy as jnp
from jax import lax
from jax.sharding import PartitionSpec as P

D = 768
PASSES = 3


def shards(points, centroids):
    factor = 1.0 / math.sqrt(D)
    logits = (
        lax.dot_general(
            points, centroids, (((1,), (1,)), ((), ())), preferred_element_type=jnp.float32
        )
        * factor
    )
    n_total = points.shape[0] * lax.axis_size("dp")
    k_total = centroids.shape[0] * lax.axis_size("cent")
    log_mass = math.log(n_total / k_total)
    row_pot = jnp.zeros((points.shape[0],), jnp.float32)
    col_pot = jnp.zeros((centroids.shape[0],), jnp.float32)
    for sweep in range(PASSES):
        shifted = logits + row_pot[:, None]
        peak = lax.pmax(jnp.max(shifted, axis=0), "dp")
        total = lax.psum(jnp.sum(jnp.exp(shifted - peak[None, :]), axis=0), "dp")
        col_pot = log_mass - (peak + jnp.log(total))
        shifted = logits + col_pot[None, :]
        peak = lax.pmax(jnp.max(shifted, axis=1), "cent")
        total = lax.psum(jnp.sum(jnp.exp(shifted - peak[:, None]), axis=1), "cent")
        row_pot = -(peak + jnp.log(total))
    weights = jnp.exp(logits + row_pot[:, None] + col_pot[None, :])
    mass = jnp.sum(weights, axis=0)
    numerator = lax.dot_general(
        weights.astype(jnp.bfloat16),
        points,
        (((0,), (0,)), ((), ())),
        preferred_element_type=jnp.float32,
    )
    numerator, mass = lax.psum((numerator, mass), "dp")
    updated = (numerator + centroids.astype(jnp.float32)) / (mass + 1.0)[:, None]
    return updated.astype(jnp.bfloat16)


def solution(mesh):
    return jax.shard_map(
        shards,
        mesh=mesh,
        in_specs=(P("dp", None), P("cent", None)),
        out_specs=P("cent", None),
        check_vma=False,
    )
```

profile of v0, /device:TPU:6, one launch (start us, length us, event | category | flops | bytes accessed | tf_op | source)
XLA Modules:
  0.0 1249.5 jit_solution(18292041778935732259)
XLA Ops:
  7.9 5.2 fusion.6
  13.1 128.3 %pmax.42 = f32[1024]{0:T(1024)S(1)} all-reduce(f32[1024]{0:T(1024)S(1)} %get-tuple-element.5), channel_id=1, replica_groups=mesh['dp'=64,'cent'=8] {'dp'}, use_global_device_ids=true, to_apply=%region_1.0 | all-reduce | flops 1024 | bytes 8192 | tf_op jit(solution)/shard_map/pmax | solution.py:27
  141.4 2.8 exponential_reduce_fusion.5
  144.2 134.8 %psum.56 = f32[1024]{0:T(1024)S(1)} all-reduce(f32[1024]{0:T(1024)S(1)} %exponential_reduce_fusion.5), channel_id=1, replica_groups=mesh['dp'=64,'cent'=8] {'dp'}, use_global_device_ids=true, to_apply=%region_3.0 | all-reduce | flops 1024 | bytes 8192 | tf_op jit(solution)/shard_map/psum | solution.py:28
  281.6 12.4 pmax.43
  294.0 3.1 exponential_reduce_fusion.4
  297.1 12.5 psum.57
  312.1 139.0 %pmax.44 = f32[1024]{0:T(1024)S(1)} all-reduce(f32[1024]{0:T(1024)S(1)} %add_reduce_fusion.3), channel_id=1, replica_groups=mesh['dp'=64,'cent'=8] {'dp'}, use_global_device_ids=true, to_apply=%region_9.0 | all-reduce | flops 1024 | bytes 8192 | tf_op jit(solution)/shard_map/pmax | solution.py:27
  451.1 2.9 exponential_reduce_fusion.3
  454.1 138.9 %psum.58 = f32[1024]{0:T(1024)S(1)} all-reduce(f32[1024]{0:T(1024)S(1)} %exponential_reduce_fusion.3), channel_id=1, replica_groups=mesh['dp'=64,'cent'=8] {'dp'}, use_global_device_ids=true, to_apply=%region_11.0 | all-reduce | flops 1024 | bytes 8192 | tf_op jit(solution)/shard_map/psum | solution.py:28
  595.6 12.4 pmax.45
  608.0 3.1 exponential_reduce_fusion.2
  611.1 12.4 psum.59
  626.1 139.0 %pmax.46 = f32[1024]{0:T(1024)S(1)} all-reduce(f32[1024]{0:T(1024)S(1)} %add_reduce_fusion.1), channel_id=1, replica_groups=mesh['dp'=64,'cent'=8] {'dp'}, use_global_device_ids=true, to_apply=%region_17.0 | all-reduce | flops 1024 | bytes 8192 | tf_op jit(solution)/shard_map/pmax | solution.py:27
  765.1 2.9 exponential_reduce_fusion.1
  768.0 138.9 %psum.60 = f32[1024]{0:T(1024)S(1)} all-reduce(f32[1024]{0:T(1024)S(1)} %exponential_reduce_fusion.1), channel_id=1, replica_groups=mesh['dp'=64,'cent'=8] {'dp'}, use_global_device_ids=true, to_apply=%region_19.0 | all-reduce | flops 1024 | bytes 8192 | tf_op jit(solution)/shard_map/psum | solution.py:28
  909.5 12.4 pmax.47
  921.9 3.1 exponential_reduce_fusion
  925.0 12.6 %psum.61 = f32[1024]{0:T(1024)S(1)} all-reduce(f32[1024]{0:T(1024)S(1)} %exponential_reduce_fusion), channel_id=1, replica_groups=mesh['dp'=64,'cent'=8] {'cent'}, use_global_device_ids=true, to_apply=%region_23.0 | all-reduce | flops 1024 | bytes 8192 | tf_op jit(solution)/shard_map/psum | solution.py:32
  937.6 5.9 fusion.2
  943.6 3.1 fusion
  946.6 139.1 %psum.63 = f32[1024]{0:T(1024)S(1)} all-reduce(f32[1024]{0:T(1024)S(1)} %fusion), channel_id=1, replica_groups=mesh['dp'=64,'cent'=8] {'dp'}, use_global_device_ids=true, to_apply=%region_26.0 | all-reduce | flops 1024 | bytes 8192 | tf_op jit(solution)/shard_map/psum | solution.py:42
  1085.7 153.5 %all-reduce.2.cloned.1.call-done = f32[1024,768]{1,0:T(8,128)} async-done(((f32[1024,768]{1,0:T(8,128)}), f32[1024,768]{1,0:T(8,128)}) %all-reduce.2.cloned.1.call-update) | async-done | bytes 3145744 | tf_op jit(solution)/shard_map/psum | solution.py:42
  1239.2 3.4 divide_convert_fusion
  (18 shorter events, 14.2 us)
Async XLA Ops:
  6.5 1.4 copy-start
  6.5 1232.7 %all-reduce.2.cloned.1.call-start = ((), (), s32[]{:S(2)}) async-start(), calls=%async_computation | async-start | bytes 6291456 | tf_op jit(solution)/shard_map/psum | solution.py:42
  943.6 295.6 %copy-start.1 = (bf16[1024,768]{1,0:T(8,128)(2,1)S(1)}, bf16[1024,768]{1,0:T(8,128)(2,1)}, u32[]{:S(2)}) copy-start(bf16[1024,768]{1,0:T(8,128)(2,1)} %param.3) | copy-start | bytes 4718596
Sparse Core Ops, SparseCore 0:
  943.7 295.4 all-reduce.1
where the time goes:
time: 1250 us
  blocking collectives  1030 us (82%)
  waiting for transfers between devices  153 us (12%)
  other arithmetic  37.1 us (3%)
  between operations  13.5 us (1%)
    psum x3, blocking collectives, shards(): total = lax.psum(jnp.sum(jnp.exp(shifted - peak[None, :]), axis=0), 'dp')  413 us
    pmax x3, blocking collectives, shards(): peak = lax.pmax(jnp.max(shifted, axis=0), 'dp')  406 us
    psum x1, waiting for transfers between devices, shards(): numerator, mass = lax.psum((numerator, mass), 'dp')  153 us
    psum x1, blocking collectives, shards(): numerator, mass = lax.psum((numerator, mass), 'dp')  139 us
    psum x3, blocking collectives, shards(): total = lax.psum(jnp.sum(jnp.exp(shifted - peak[:, None]), axis=1), 'cent')  37.5 us
    pmax x3, blocking collectives, shards(): peak = lax.pmax(jnp.max(shifted, axis=1), 'cent')  37.3 us
  transfers between devices with their start and end apart: 1, of which 1 were waited for; matrix products, arithmetic and copies ran while one was open for 0% of the time, Pallas kernels for 0%

commit v1 on v0

v1 whole, which is shorter than its diff:
```python
import functools
import math

import jax
import jax.numpy as jnp
from jax import lax
from jax.experimental import pallas as pl
from jax.experimental.pallas import tpu as pltpu
from jax.sharding import PartitionSpec as P

NX, NZ, NC = 4, 16, 8
LANES = 128
MESH = pl.DeviceIdType.MESH
FAR = [8, 7, 9, 6, 10, 5, 11, 4, 12, 3, 13, 2, 14, 1, 15]
NEAR = FAR[::-1]


def aligned(start, size):
    return pl.ds(pl.multiple_of(start, size), size)


def to_rows(wide, tiles):
    return jnp.concatenate(
        [wide[:, t * LANES : (t + 1) * LANES] for t in range(tiles)], axis=0
    )


def to_wide(rows, tiles):
    return jnp.concatenate([rows[t : t + 1, :] for t in range(tiles)], axis=1)


def kernel(
    log_mass, factor,
    p_ref, c_ref, o_ref,
    mat, scale, num, total, part,
    vec, cx, cz, rc, mx, nx, nz,
    vec_send, cx_recv, cz_recv, rc_recv, nx_send, nx_recv, nz_send, nz_recv, ag_send, agz_recv, agx_recv,
):
    npts, depth = p_ref.shape
    ncent = c_ref.shape[0]
    rt, ct = npts // LANES, ncent // LANES
    per_x, per = ncent // NX, ncent // (NX * NZ)

    dp = lax.axis_index("dp")
    cent = lax.axis_index("cent")
    x, z = dp // NZ, dp % NZ

    def x_peer(k):
        return {"dp": ((x + k) % NX) * NZ + z}

    def z_peer(k):
        return {"dp": x * NZ + (z + k) % NZ}

    def c_peer(k):
        return {"cent": (cent + k) % NC}

    x_peers = [x_peer(k) for k in range(1, NX)]
    z_peers = [z_peer(k) for k in range(1, NZ)]
    c_peers = [c_peer(k) for k in range(1, NC)]

    barrier = pltpu.get_barrier_semaphore()
    for peer in x_peers + z_peers + c_peers:
        pl.semaphore_signal(barrier, inc=1, device_id=peer, device_id_type=MESH)

    def swap(slot, rows, peers, land, recv):
        for k, peer in enumerate(peers):
            pltpu.make_async_remote_copy(
                src_ref=vec.at[slot, pl.ds(0, rows)],
                dst_ref=land.at[k, pl.ds(0, rows)],
                send_sem=vec_send.at[slot],
                recv_sem=recv,
                device_id=peer,
                device_id_type=MESH,
            ).start()

    def landed(land, recv):
        pltpu.make_async_copy(land, land, recv).wait()

    def merge(slot, land, count, tiles):
        peak = vec[slot, :tiles]
        for k in range(count):
            peak = jnp.maximum(peak, land[k, :tiles])
        acc = vec[slot, tiles : 2 * tiles] * jnp.exp(vec[slot, :tiles] - peak)
        for k in range(count):
            acc += land[k, tiles : 2 * tiles] * jnp.exp(land[k, :tiles] - peak)
        return peak, acc

    def add_up(slot, land, count, tiles):
        acc = vec[slot, :tiles]
        for k in range(count):
            acc += land[k, :tiles]
        return acc

    def spread(rows, tiles):
        for t in range(tiles):
            wide = jnp.broadcast_to(rows[t : t + 1, :], (LANES, LANES))
            scale[t * LANES : (t + 1) * LANES, :] = wide.T

    def column_sums():
        def step(r, acc):
            rows = aligned(r * LANES, LANES)
            by = scale[rows, :]
            out = []
            for t in range(ct):
                v = mat[rows, t * LANES : (t + 1) * LANES] * by
                out.append(acc[t] + jnp.sum(v.reshape(LANES // 8, 8, LANES), axis=0))
            return tuple(out)

        zero = tuple(jnp.zeros((8, LANES), jnp.float32) for _ in range(ct))
        acc = lax.fori_loop(0, rt, step, zero)
        return jnp.concatenate([jnp.sum(a, axis=0, keepdims=True) for a in acc], axis=0)

    def row_sums(wide):
        def step(r, carry):
            rows = aligned(r * LANES, LANES)
            acc = mat[rows, :LANES] * wide[:, :LANES]
            for t in range(1, ct):
                acc += mat[rows, t * LANES : (t + 1) * LANES] * wide[:, t * LANES : (t + 1) * LANES]
            part[pl.ds(r, 1), :] = jnp.sum(acc.T, axis=0, keepdims=True)
            return carry

        lax.fori_loop(0, rt, step, 0)

    def logits_step(r, peak):
        rows = aligned(r * 256, 256)
        got = factor * lax.dot_general(
            p_ref[rows, :], c_ref[...], (((1,), (1,)), ((), ())), preferred_element_type=jnp.float32
        )
        mat[rows, :] = got
        return jnp.maximum(peak, jnp.max(got.reshape(32, 8, ncent), axis=0))

    peak8 = lax.fori_loop(
        0, npts // 256, logits_step, jnp.full((8, ncent), -jnp.inf, jnp.float32)
    )
    peak = jnp.max(peak8, axis=0, keepdims=True)

    def first_sum(r, acc):
        rows = aligned(r * LANES, LANES)
        got = jnp.exp(mat[rows, :] - peak)
        return acc + jnp.sum(got.reshape(LANES // 8, 8, ncent), axis=0)

    acc = lax.fori_loop(0, rt, first_sum, jnp.zeros((8, ncent), jnp.float32))
    vec[0, :ct] = to_rows(peak, ct)
    vec[0, ct : 2 * ct] = to_rows(jnp.sum(acc, axis=0, keepdims=True), ct)

    pl.semaphore_wait(barrier, NX + NZ + NC - 3)

    swap(0, 2 * ct, x_peers, cx.at[0], cx_recv.at[0])
    landed(cx.at[0], cx_recv.at[0])
    m, s = merge(0, cx.at[0], NX - 1, ct)
    vec[1, :ct] = m
    vec[1, ct : 2 * ct] = s
    swap(1, 2 * ct, z_peers, cz.at[0], cz_recv.at[0])
    landed(cz.at[0], cz_recv.at[0])
    m, s = merge(1, cz.at[0], NZ - 1, ct)
    col_pot = to_wide(log_mass - (m + jnp.log(s)), ct)

    def first_rows(r, carry):
        rows = aligned(r * LANES, LANES)
        got = mat[rows, :] + col_pot
        top = got[:, :LANES]
        for t in range(1, ct):
            top = jnp.maximum(top, got[:, t * LANES : (t + 1) * LANES])
        top = jnp.max(top, axis=1, keepdims=True)
        got = jnp.exp(got - top)
        mat[rows, :] = got
        acc = got[:, :LANES]
        for t in range(1, ct):
            acc += got[:, t * LANES : (t + 1) * LANES]
        part[pl.ds(r, 1), :] = jnp.sum(acc.T, axis=0, keepdims=True)
        vec[2, pl.ds(r, 1), :] = jnp.broadcast_to(top, (LANES, LANES)).T[:1, :]
        return carry

    lax.fori_loop(0, rt, first_rows, 0)
    vec[2, rt : 2 * rt] = part[...]
    swap(2, 2 * rt, c_peers, rc.at[0], rc_recv.at[0])
    landed(rc.at[0], rc_recv.at[0])
    m, s = merge(2, rc.at[0], NC - 1, rt)
    u = jnp.exp(vec[2, :rt] - (m + jnp.log(s)))
    v = None
    spread(u, rt)

    slot = 3
    for sweep in (1, 2):
        vec[slot, :ct] = column_sums()
        swap(slot, ct, x_peers, cx.at[sweep, :, pl.ds(0, ct)], cx_recv.at[sweep])
        landed(cx.at[sweep, :, pl.ds(0, ct)], cx_recv.at[sweep])
        vec[slot + 1, :ct] = add_up(slot, cx.at[sweep], NX - 1, ct)
        swap(slot + 1, ct, z_peers, cz.at[sweep, :, pl.ds(0, ct)], cz_recv.at[sweep])
        landed(cz.at[sweep, :, pl.ds(0, ct)], cz_recv.at[sweep])
        v = math.exp(log_mass) / add_up(slot + 1, cz.at[sweep], NZ - 1, ct)
        row_sums(to_wide(v, ct))
        vec[slot + 2, :rt] = u * part[...]
        swap(slot + 2, rt, c_peers, rc.at[sweep, :, pl.ds(0, rt)], rc_recv.at[sweep])
        landed(rc.at[sweep, :, pl.ds(0, rt)], rc_recv.at[sweep])
        u = u / add_up(slot + 2, rc.at[sweep], NC - 1, rt)
        spread(u, rt)
        slot += 3

    vec[slot, :ct] = v * column_sums()
    swap(slot, ct, x_peers, mx.at[pl.ds(0, NX - 1)], cx_recv.at[3])
    for t in range(ct):
        total[t : t + 1, :] = v[t : t + 1, :]

    def to_x(j, to):
        rows = ((to * NZ + (z + j) % NZ)) * per
        return num.at[aligned(rows, per)]

    for k in (2, 1, 3, 0):
        to = (x + k) % NX
        cols = aligned(to * per_x, per_x)
        wide = to_wide(total[pl.ds(to * (per_x // LANES), per_x // LANES), :], per_x // LANES)
        weights = []
        for r in range(rt):
            by = scale[r * LANES : (r + 1) * LANES, :]
            got = mat[r * LANES : (r + 1) * LANES, cols]
            weights.append(
                jnp.concatenate(
                    [
                        got[:, t * LANES : (t + 1) * LANES] * by * wide[:, t * LANES : (t + 1) * LANES]
                        for t in range(per_x // LANES)
                    ],
                    axis=1,
                ).astype(jnp.bfloat16)
            )
        num[cols, :] = lax.dot_general(
            jnp.concatenate(weights, axis=0), p_ref[...],
            (((0,), (0,)), ((), ())), preferred_element_type=jnp.float32,
        )
        if k:
            for j in FAR + [0]:
                pltpu.make_async_remote_copy(
                    src_ref=to_x(j, to),
                    dst_ref=nx.at[j, k - 1],
                    send_sem=nx_send,
                    recv_sem=nx_recv.at[j],
                    device_id=x_peer(k),
                    device_id_type=MESH,
                ).start()

    landed(mx.at[pl.ds(0, NX - 1)], cx_recv.at[3])
    vec[slot + 1, :ct] = add_up(slot, mx, NX - 1, ct)
    swap(slot + 1, ct, z_peers, mx.at[pl.ds(NX - 1, NZ - 1)], cz_recv.at[3])

    for j in FAR + [0]:
        landed(nx.at[j], nx_recv.at[j])
        mine = to_x(j, x)
        mine[...] = mine[...] + nx[j, 0] + nx[j, 1] + nx[j, 2]
        if j:
            pltpu.make_async_remote_copy(
                src_ref=mine,
                dst_ref=nz.at[j - 1],
                send_sem=nz_send,
                recv_sem=nz_recv,
                device_id=z_peer(j),
                device_id_type=MESH,
            ).start()

    landed(mx.at[pl.ds(NX - 1, NZ - 1)], cz_recv.at[3])
    mass = vec[slot + 1, :ct]
    for k in range(NX - 1, NX + NZ - 2):
        mass += mx[k]
    total[...] = mass
    first = (x * NZ + z) * per
    row = total[pl.ds(first // LANES, 1), :]
    scale[:LANES, :] = jnp.broadcast_to(row, (LANES, LANES)).T
    mass = scale[aligned(first % LANES, per), :][:, :1]

    landed(nz, nz_recv)
    own = aligned(first, per)
    acc = num[own, :]
    for k in range(NZ - 1):
        acc += nz[k]
    acc = (acc + c_ref[own, :].astype(jnp.float32)) / (mass + 1.0)
    o_ref[own, :] = acc.astype(o_ref.dtype)

    def send_rows(rows, peer, recv):
        pltpu.make_async_remote_copy(
            src_ref=o_ref.at[rows], dst_ref=o_ref.at[rows],
            send_sem=ag_send, recv_sem=recv, device_id=peer, device_id_type=MESH,
        ).start()

    for j in FAR:
        send_rows(own, z_peer(j), agz_recv.at[j - 1])
    for j in [0] + NEAR:
        rows = aligned((x * NZ + (z + NZ - j) % NZ) * per, per)
        if j:
            landed(o_ref.at[rows], agz_recv.at[j - 1])
        for k in (2, 1, 3):
            send_rows(rows, x_peer(k), agx_recv)

    rest = o_ref.at[pl.ds(0, (NX - 1) * per_x)]
    landed(rest, agx_recv)

    for sweep in range(3):
        rows = 2 * ct if sweep == 0 else ct
        landed(cx.at[sweep, :, pl.ds(0, rows)], vec_send.at[3 * sweep])
        landed(cz.at[sweep, :, pl.ds(0, rows)], vec_send.at[3 * sweep + 1])
        landed(rc.at[sweep, :, pl.ds(0, rows)], vec_send.at[3 * sweep + 2])
    landed(mx.at[pl.ds(0, NX - 1)], vec_send.at[slot])
    landed(mx.at[pl.ds(NX - 1, NZ - 1)], vec_send.at[slot + 1])
    landed(num.at[pl.ds(0, (NX - 1) * per_x)], nx_send)
    landed(nz, nz_send)
    landed(o_ref.at[pl.ds(0, (NZ - 1) * per)], ag_send)
    landed(rest, ag_send)


def shards(points, centroids):
    npts, depth = points.shape
    ncent = centroids.shape[0]
    n_total = npts * lax.axis_size("dp")
    k_total = ncent * lax.axis_size("cent")
    tiles = max(npts, ncent) // LANES
    per = ncent // (NX * NZ)
    f32 = jnp.float32
    vmem = pl.BlockSpec(memory_space=pltpu.VMEM)
    dma = pltpu.SemaphoreType.DMA
    return pl.pallas_call(
        functools.partial(kernel, math.log(n_total / k_total), 1.0 / math.sqrt(depth)),
        out_shape=jax.ShapeDtypeStruct((ncent, depth), jnp.bfloat16),
        in_specs=[vmem, vmem],
        out_specs=vmem,
        scratch_shapes=[
            pltpu.VMEM((npts, ncent), f32),
            pltpu.VMEM((max(npts, ncent), LANES), f32),
            pltpu.VMEM((ncent, depth), f32),
            pltpu.VMEM((tiles, LANES), f32),
            pltpu.VMEM((npts // LANES, LANES), f32),
            pltpu.VMEM((11, 2 * tiles, LANES), f32),
            pltpu.VMEM((3, NX - 1, 2 * tiles, LANES), f32),
            pltpu.VMEM((3, NZ - 1, 2 * tiles, LANES), f32),
            pltpu.VMEM((3, NC - 1, 2 * tiles, LANES), f32),
            pltpu.VMEM((NX + NZ - 2, ncent // LANES, LANES), f32),
            pltpu.VMEM((NZ, NX - 1, per, depth), f32),
            pltpu.VMEM((NZ - 1, per, depth), f32),
            dma((11,)), dma((4,)), dma((4,)), dma((3,)),
            dma, dma((NZ,)), dma, dma, dma, dma((NZ - 1,)), dma,
        ],
        compiler_params=pltpu.CompilerParams(
            collective_id=0, has_side_effects=True, vmem_limit_bytes=48 * 2**20
        ),
        cost_estimate=pl.CostEstimate(
            flops=4 * npts * ncent * depth, transcendentals=2 * npts * ncent,
            bytes_accessed=2 * (npts + 2 * ncent) * depth,
        ),
        name="balance",
    )(points, centroids)


def solution(mesh):
    return jax.shard_map(
        shards,
        mesh=mesh,
        in_specs=(P("dp", None), P("cent", None)),
        out_specs=P("cent", None),
        check_vma=False,
    )
```

time: 1250 us -> 166 us (0.13)
  blocking collectives: 1030 us -> 0 us
  Pallas kernels: 0 us -> 161 us
  waiting for transfers between devices: 153 us -> 0 us
  other arithmetic: 37.1 us -> 0 us
  between operations: 13.5 us -> 0.01 us
    psum x7 -> x0, blocking collectives: 589 us -> none  [the longest x3 413 us: shards(): total = lax.psum(jnp.sum(jnp.exp(shifted - peak[None, :]), axis=0), 'dp')]
    pmax x6 -> x0, blocking collectives: 444 us -> none  [the longest x3 406 us: shards(): peak = lax.pmax(jnp.max(shifted, axis=0), 'dp')]
    pallas_call x0 -> x1, Pallas kernels: none -> 161 us  [shards(): pl.pallas_call(functools.partial(kernel, math.log(n_total / k_total), 1.0...]
    psum x1 -> x0, waiting for transfers between devices: 153 us -> none  [shards(): numerator, mass = lax.psum((numerator, mass), 'dp')]
    reduce_sum x7 -> x0, other arithmetic: 20.9 us -> none  [the longest x3 9.19 us: shards(): total = lax.psum(jnp.sum(jnp.exp(shifted - peak[:, None]), axis=1), 'cent')]
    reduce_max x5 -> x0, other arithmetic: 12.7 us -> none  [the longest x3 7.62 us: shards(): peak = lax.pmax(jnp.max(shifted, axis=1), 'cent')]
  transfers between devices with their start and end apart: 1 -> 0, of which waited for: 1 -> 0; matrix products, arithmetic and copies ran while one was open for 0% -> 0% of each run, Pallas kernels for 0% -> 0%
where the time goes in v1:
time: 166 us; the launch traced here: 165 us
  Pallas kernels  161 us (97%)
  local copies, waits for them, and re-layouts  3.96 us (2%)
    pallas_call x1, Pallas kernels, shards(): pl.pallas_call(functools.partial(kernel, math.log(n_total / k_total), 1.0...  161 us
    unnamed x5, local copies, waits for them, and re-layouts  3.96 us

profile of v1, /device:TPU:6, one launch (start us, length us, event | category | flops | bytes accessed | tf_op | source)
XLA Modules:
  0.0 164.9 jit_solution(5443700749638814682)
XLA Ops:
  0.0 0.0 copy-start
  0.0 1.4 copy-done
  1.4 0.0 copy-start.1
  1.4 1.4 copy-done.1
  2.8 161.0 %balance.1 = bf16[1024,768]{1,0:T(8,128)(2,1)S(1)} custom-call(bf16[1024,768]{1,0:T(8,128)(2,1)S(1)} %copy-done, bf16[1024,768]{1,0:T(8,128)(2,1)S(1)} %copy-done.1), custom_call_target="tpu_custom_call" | custom-call | flops 3221225472 | bytes 4718592 | tf_op jit(solution)/shard_map/balance/pallas_call | solution.py:318
  163.8 1.1 copy.4
Async XLA Ops:
  0.0 1.4 copy-start
  1.4 1.4 copy-start.1

commit v2 on v0

v2 whole, which is shorter than its diff:
```python
import functools
import math

import jax
import jax.numpy as jnp
from jax import lax
from jax.experimental import pallas as pl
from jax.experimental.pallas import tpu as pltpu
from jax.sharding import PartitionSpec as P

NX, NZ, NC = 4, 16, 8
LANES = 128
MESH = pl.DeviceIdType.MESH
FAR = [8, 7, 9, 6, 10, 5, 11, 4, 12, 3, 13, 2, 14, 1, 15]
NEAR = [3, 13, 2, 14, 1, 15]
BY_RELAY = [8, 9, 7, 10, 6, 11, 5]
LANDING = [0, 4, 12, 1, 15, 2, 14, 3, 13, 5, 11, 6, 10, 7, 9, 8]


def aligned(start, size):
    return pl.ds(pl.multiple_of(start, size), size)


def to_rows(wide, tiles):
    return jnp.concatenate(
        [wide[:, t * LANES : (t + 1) * LANES] for t in range(tiles)], axis=0
    )


def to_wide(rows, tiles):
    return jnp.concatenate([rows[t : t + 1, :] for t in range(tiles)], axis=1)


def kernel(
    log_mass, factor,
    p_hbm, c_hbm, o_ref,
    p_ref, c_ref, pts, mat, scale, tile, num, total, part, top, cpot,
    vec, cx, cz, rc, px, mass_out, mass_in, nz,
    in_sem, pts_send, pts_recv, pair_send, pair_recv,
    vec_send, cx_recv, cz_recv, rc_recv, px_recv, mass_send, mass_recv,
    nz_send, nz_recv, ag_send, agz_recv, agl_recv, agr_recv, agx_recv,
):
    npts, depth = p_ref.shape
    ncent = c_ref.shape[0]
    rt, ct = npts // LANES, ncent // LANES
    per_x, per = ncent // NX, ncent // (NX * NZ)
    qt = per_x // LANES
    half = npts // 2
    f32 = jnp.float32

    dp = lax.axis_index("dp")
    cent = lax.axis_index("cent")
    x, z = dp // NZ, dp % NZ
    core = cent % 2

    def x_peer(k):
        return {"dp": ((x + k) % NX) * NZ + z}

    def z_peer(k):
        return {"dp": x * NZ + (z + k) % NZ}

    def c_peer(k):
        return {"cent": (cent + k) % NC}

    sibling = {"cent": cent + 1 - 2 * core}
    x_peers = [x_peer(k) for k in range(1, NX)]
    z_peers = [z_peer(k) for k in range(1, NZ)]
    c_peers = [c_peer(k) for k in range(1, NC)]

    c_in = pltpu.make_async_copy(c_hbm, c_ref, in_sem.at[4])
    c_in.start()
    p_in = []
    for r in range(4):
        rows = pl.ds(r * (npts // 4), npts // 4)
        p_in.append(pltpu.make_async_copy(p_hbm.at[rows], p_ref.at[rows], in_sem.at[r]))
        p_in[-1].start()

    barrier = pltpu.get_barrier_semaphore()
    for peer in x_peers + z_peers + c_peers:
        pl.semaphore_signal(barrier, inc=1, device_id=peer, device_id_type=MESH)

    pending = []

    def send(src, dst, send_sem, recv_sem, peer):
        pltpu.make_async_remote_copy(
            src_ref=src, dst_ref=dst, send_sem=send_sem, recv_sem=recv_sem,
            device_id=peer, device_id_type=MESH,
        ).start()

    def landed(land, recv):
        pltpu.make_async_copy(land, land, recv).wait()

    def drain():
        for land, sem in pending:
            landed(land, sem)

    def swap(src, peers, land, send_sem, recv, order=None):
        for k in order or range(1, len(peers) + 1):
            send(src, land.at[k - 1], send_sem, recv, peers[k - 1])
        pending.append((land, send_sem))

    def merge(own, land, count):
        peak = own
        for k in range(count):
            peak = jnp.maximum(peak, land[k])
        acc = jnp.exp(own - peak)
        for k in range(count):
            acc += jnp.exp(land[k] - peak)
        return peak + jnp.log(acc)

    def add_up(own, land, count):
        acc = own
        for k in range(count):
            acc += land[k]
        return acc

    def spread(rows, out, tiles):
        for t in range(tiles):
            wide = jnp.broadcast_to(rows[t : t + 1, :], (LANES, LANES))
            out[t * LANES : (t + 1) * LANES, :] = wide.T

    def column_sums():
        def step(r, acc):
            rows = aligned(r * LANES, LANES)
            by = scale[rows, :]
            out = []
            for t in range(ct):
                v = mat[rows, t * LANES : (t + 1) * LANES] * by
                out.append(acc[t] + jnp.sum(v.reshape(LANES // 8, 8, LANES), axis=0))
            return tuple(out)

        zero = tuple(jnp.zeros((8, LANES), f32) for _ in range(ct))
        acc = lax.fori_loop(0, rt, step, zero)
        return jnp.concatenate([jnp.sum(a, axis=0, keepdims=True) for a in acc], axis=0)

    def row_sums(wide):
        def step(r, carry):
            rows = aligned(r * LANES, LANES)
            acc = mat[rows, :LANES] * wide[:, :LANES]
            for t in range(1, ct):
                acc += mat[rows, t * LANES : (t + 1) * LANES] * wide[:, t * LANES : (t + 1) * LANES]
            part[pl.ds(r, 1), :] = jnp.sum(acc.T, axis=0, keepdims=True)
            return carry

        lax.fori_loop(0, rt, step, 0)

    c_in.wait()
    peak8 = jnp.full((8, ncent), -jnp.inf, f32)
    for r in range(4):
        p_in[r].wait()
        rows = pl.ds(r * (npts // 4), npts // 4)
        got = factor * lax.dot_general(
            p_ref[rows, :], c_ref[...], (((1,), (1,)), ((), ())), preferred_element_type=f32
        )
        mat[rows, :] = got
        peak8 = jnp.maximum(peak8, jnp.max(got.reshape(npts // 32, 8, ncent), axis=0))
    peak = jnp.max(peak8, axis=0, keepdims=True)

    def first_sum(r, acc):
        rows = aligned(r * LANES, LANES)
        got = jnp.exp(mat[rows, :] - peak)
        return acc + jnp.sum(got.reshape(LANES // 8, 8, ncent), axis=0)

    acc = lax.fori_loop(0, rt, first_sum, jnp.zeros((8, ncent), f32))
    vec[0] = to_rows(peak + jnp.log(jnp.sum(acc, axis=0, keepdims=True)), ct)

    pl.semaphore_wait(barrier, NX + NZ + NC - 3)

    swap(vec.at[0], x_peers, cx.at[0], vec_send.at[0], cx_recv.at[0])

    mine = aligned(core * half, half)
    for k in (1, 3, 2):
        send(p_ref.at[mine], pts.at[k - 1, mine], pts_send, pts_recv.at[k - 1], x_peers[k - 1])
    pending.append((pts.at[:, mine], pts_send))

    def pass_on(k):
        landed(pts.at[k - 1, mine], pts_recv.at[k - 1])
        send(pts.at[k - 1, mine], pts.at[k - 1, mine], pair_send, pair_recv, sibling)

    landed(cx.at[0], cx_recv.at[0])
    vec[1] = merge(vec[0], cx.at[0], NX - 1)
    swap(vec.at[1], z_peers, cz.at[0], vec_send.at[1], cz_recv.at[0], FAR)
    landed(cz.at[0], cz_recv.at[0])
    col_pot = log_mass - merge(vec[1], cz.at[0], NZ - 1)
    wide_pot = to_wide(col_pot, ct)

    def first_rows(r, carry):
        rows = aligned(r * LANES, LANES)
        got = mat[rows, :] + wide_pot
        high = got[:, :LANES]
        for t in range(1, ct):
            high = jnp.maximum(high, got[:, t * LANES : (t + 1) * LANES])
        high = jnp.max(high, axis=1, keepdims=True)
        got = jnp.exp(got - high)
        mat[rows, :] = got
        acc = got[:, :LANES]
        for t in range(1, ct):
            acc += got[:, t * LANES : (t + 1) * LANES]
        part[pl.ds(r, 1), :] = jnp.sum(acc.T, axis=0, keepdims=True)
        top[pl.ds(r, 1), :] = jnp.broadcast_to(high, (LANES, LANES)).T[:1, :]
        return carry

    lax.fori_loop(0, rt, first_rows, 0)
    vec[2] = top[...] + jnp.log(part[...])
    swap(vec.at[2], c_peers, rc.at[0], vec_send.at[2], rc_recv.at[0])
    landed(rc.at[0], rc_recv.at[0])
    row_pot = -merge(vec[2], rc.at[0], NC - 1)
    u = jnp.exp(top[...] + row_pot)
    spread(u, scale, rt)

    for sweep in (1, 2):
        at = 3 * sweep
        vec[at] = column_sums()
        swap(vec.at[at], x_peers, cx.at[sweep], vec_send.at[at], cx_recv.at[sweep])
        landed(cx.at[sweep], cx_recv.at[sweep])
        vec[at + 1] = add_up(vec[at], cx.at[sweep], NX - 1)
        swap(vec.at[at + 1], z_peers, cz.at[sweep], vec_send.at[at + 1], cz_recv.at[sweep], FAR)
        if sweep == 1:
            pass_on(1)
            pass_on(3)
        else:
            pass_on(2)
            pending.append((pts.at[:, mine], pair_send))
            landed(pts.at[:, aligned(half - core * half, half)], pair_recv)
            quarter = c_ref[aligned(x * per_x, per_x), :]
            for k in range(NX):
                tile[:, k * npts : (k + 1) * npts] = factor * lax.dot_general(
                    quarter, p_ref[...] if k == 0 else pts[k - 1],
                    (((1,), (1,)), ((), ())), preferred_element_type=f32,
                )
            landed(px.at[0], px_recv.at[0])
        landed(cz.at[sweep], cz_recv.at[sweep])
        v = math.exp(log_mass) / add_up(vec[at + 1], cz.at[sweep], NZ - 1)
        row_sums(to_wide(v, ct))
        vec[at + 2] = u * part[...]
        swap(vec.at[at + 2], c_peers, rc.at[sweep], vec_send.at[at + 2], rc_recv.at[sweep])
        if sweep == 2:
            total[...] = col_pot + jnp.log(v)
            spread(total[pl.ds(x * qt, qt), :], cpot, qt)
            for k in range(NX):
                pot = vec[9] if k == 0 else px[0, k - 1]
                for t in range(rt):
                    cols = slice(k * npts + t * LANES, k * npts + (t + 1) * LANES)
                    tile[:, cols] = jnp.exp(tile[:, cols] + (cpot[...] + pot[t : t + 1, :]))
        landed(rc.at[sweep], rc_recv.at[sweep])
        got = add_up(vec[at + 2], rc.at[sweep], NC - 1)
        if sweep == 1:
            u = u / got
            vec[9] = row_pot - jnp.log(got)
            swap(vec.at[9], x_peers, px.at[0], vec_send.at[9], px_recv.at[0])
            spread(u, scale, rt)
        else:
            vec[10] = 1.0 / got
            swap(vec.at[10], x_peers, px.at[1], vec_send.at[10], px_recv.at[1])
            landed(px.at[1], px_recv.at[1])

    mass = jnp.zeros((per_x, LANES), f32)
    acc = jnp.zeros((per_x, depth), f32)
    for k in range(NX):
        by = vec[10] if k == 0 else px[1, k - 1]
        weights = []
        for t in range(rt):
            got = tile[:, k * npts + t * LANES : k * npts + (t + 1) * LANES] * by[t : t + 1, :]
            mass += got
            weights.append(got.astype(jnp.bfloat16))
        acc += jnp.dot(
            jnp.concatenate(weights, axis=1), p_ref[...] if k == 0 else pts[k - 1],
            preferred_element_type=f32,
        )
    num[...] = acc

    def piece(j):
        return num.at[aligned(((z + j) % NZ) * per, per)]

    for j in BY_RELAY:
        by = j - 4 if j < 8 else j + 4
        send(piece(j), nz.at[j - 1], nz_send, nz_recv.at[1 if j < 8 else 2], z_peers[by - 1])
    for j in NEAR:
        send(piece(j), nz.at[j - 1], nz_send, nz_recv.at[0], z_peers[j - 1])
    for t in range(qt):
        mass_out[t : t + 1, :] = jnp.sum(mass[t * LANES : (t + 1) * LANES, :].T, axis=0, keepdims=True)
    swap(mass_out, z_peers, mass_in, mass_send, mass_recv, FAR)
    for j, group, slots in ((4, 1, (5, 6, 7)), (12, 2, (8, 9, 10, 11))):
        landed(nz.at[pl.ds(slots[0] - 1, len(slots))], nz_recv.at[group])
        here = piece(j)
        acc = here[...]
        for i in slots:
            acc += nz[i - 1]
        here[...] = acc
        send(here, nz.at[j - 1], nz_send, nz_recv.at[0], z_peers[j - 1])
    pending.append((nz, nz_send))

    landed(mass_in, mass_recv)
    total[:qt, :] = add_up(mass_out[...], mass_in, NZ - 1)
    row = total[pl.ds(z * per // LANES, 1), :]
    scale[:LANES, :] = jnp.broadcast_to(row, (LANES, LANES)).T
    mass = scale[aligned((z * per) % LANES, per), :][:, :1]

    landed(nz.at[pl.ds(0, 8)], nz_recv.at[0])
    acc = piece(0)[...]
    for j in NEAR + [4, 12]:
        acc += nz[j - 1]
    own = aligned((x * NZ + z) * per, per)
    acc = (acc + c_ref[own, :].astype(f32)) / (mass + 1.0)
    o_ref[own, :] = acc.astype(o_ref.dtype)

    def rows_of(i, j):
        return o_ref.at[aligned((((x + i) % NX) * NZ + (z + NZ - j) % NZ) * per, per)]

    def hand_on(rows, recv, peer):
        send(rows, rows, ag_send, recv, peer)

    for j in (4, 12, 1, 15, 2, 14, 3, 13):
        hand_on(rows_of(0, 0), agz_recv.at[j], z_peers[j - 1])

    def relay(n):
        j = LANDING[n]
        if n % 2:
            landed(rows_of(1, j), agr_recv.at[j])
            hand_on(rows_of(1, j), agx_recv, x_peers[2])
        else:
            landed(rows_of(3, j), agl_recv.at[j])
            hand_on(rows_of(3, j), agx_recv, x_peers[0])

    lag = 2
    for n, j in enumerate(LANDING):
        rows = rows_of(0, j)
        if j:
            landed(rows, agz_recv.at[j])
        if j == 4:
            for a in (4, 3, 2, 1):
                hand_on(rows, agz_recv.at[4 + a], z_peers[a - 1])
        if j == 12:
            for a in (3, 2, 1):
                hand_on(rows, agz_recv.at[12 - a], z_peers[NZ - a - 1])
        hand_on(rows, agx_recv if n % 2 else agl_recv.at[j], x_peers[0])
        hand_on(rows, agr_recv.at[j] if n % 2 else agx_recv, x_peers[2])
        if n >= lag:
            relay(n - lag)
    for n in range(NZ - lag, NZ):
        relay(n)
    landed(o_ref.at[pl.ds(0, 2 * NZ * per)], agx_recv)
    pending.append((o_ref.at[pl.ds(0, (4 * NZ - 1) * per)], ag_send))

    drain()


def shards(points, centroids):
    npts, depth = points.shape
    ncent = centroids.shape[0]
    n_total = npts * lax.axis_size("dp")
    k_total = ncent * lax.axis_size("cent")
    rt, ct = npts // LANES, ncent // LANES
    per_x, per = ncent // NX, ncent // (NX * NZ)
    f32, bf16 = jnp.float32, jnp.bfloat16
    vmem = pl.BlockSpec(memory_space=pltpu.VMEM)
    hbm = pl.BlockSpec(memory_space=pl.ANY)
    dma = pltpu.SemaphoreType.DMA
    return pl.pallas_call(
        functools.partial(kernel, math.log(n_total / k_total), 1.0 / math.sqrt(depth)),
        out_shape=jax.ShapeDtypeStruct((ncent, depth), bf16),
        in_specs=[hbm, hbm],
        out_specs=vmem,
        scratch_shapes=[
            pltpu.VMEM((npts, depth), bf16),
            pltpu.VMEM((ncent, depth), bf16),
            pltpu.VMEM((NX - 1, npts, depth), bf16),
            pltpu.VMEM((npts, ncent), f32),
            pltpu.VMEM((npts, LANES), f32),
            pltpu.VMEM((per_x, NX * npts), f32),
            pltpu.VMEM((per_x, depth), f32),
            pltpu.VMEM((ct, LANES), f32),
            pltpu.VMEM((rt, LANES), f32),
            pltpu.VMEM((rt, LANES), f32),
            pltpu.VMEM((per_x, LANES), f32),
            pltpu.VMEM((11, ct, LANES), f32),
            pltpu.VMEM((3, NX - 1, ct, LANES), f32),
            pltpu.VMEM((3, NZ - 1, ct, LANES), f32),
            pltpu.VMEM((3, NC - 1, rt, LANES), f32),
            pltpu.VMEM((2, NX - 1, rt, LANES), f32),
            pltpu.VMEM((per_x // LANES, LANES), f32),
            pltpu.VMEM((NZ - 1, per_x // LANES, LANES), f32),
            pltpu.VMEM((NZ - 1, per, depth), f32),
            dma((5,)), dma, dma((NX - 1,)), dma, dma,
            dma((11,)), dma((3,)), dma((3,)), dma((3,)), dma((2,)), dma, dma,
            dma, dma((3,)), dma, dma((NZ,)), dma((NZ,)), dma((NZ,)), dma,
        ],
        compiler_params=pltpu.CompilerParams(
            collective_id=0, has_side_effects=True, vmem_limit_bytes=48 * 2**20
        ),
        cost_estimate=pl.CostEstimate(
            flops=6 * npts * ncent * depth, transcendentals=3 * npts * ncent,
            bytes_accessed=2 * (npts + 2 * ncent) * depth,
        ),
        name="balance",
    )(points, centroids)


def solution(mesh):
    return jax.shard_map(
        shards,
        mesh=mesh,
        in_specs=(P("dp", None), P("cent", None)),
        out_specs=P("cent", None),
        check_vma=False,
    )
```

time: 1250 us -> 143 us (0.11)
  blocking collectives: 1030 us -> 0 us
  waiting for transfers between devices: 153 us -> 0 us
  Pallas kernels: 0 us -> 138 us
  other arithmetic: 37.1 us -> 0 us
  between operations: 13.5 us -> 0.01 us
    psum x7 -> x0, blocking collectives: 589 us -> none  [the longest x3 413 us: shards(): total = lax.psum(jnp.sum(jnp.exp(shifted - peak[None, :]), axis=0), 'dp')]
    pmax x6 -> x0, blocking collectives: 444 us -> none  [the longest x3 406 us: shards(): peak = lax.pmax(jnp.max(shifted, axis=0), 'dp')]
    psum x1 -> x0, waiting for transfers between devices: 153 us -> none  [shards(): numerator, mass = lax.psum((numerator, mass), 'dp')]
    pallas_call x0 -> x1, Pallas kernels: none -> 138 us  [shards(): pl.pallas_call(functools.partial(kernel, math.log(n_total / k_total), 1.0...]
    reduce_sum x7 -> x0, other arithmetic: 20.9 us -> none  [the longest x3 9.19 us: shards(): total = lax.psum(jnp.sum(jnp.exp(shifted - peak[:, None]), axis=1), 'cent')]
    reduce_max x5 -> x0, other arithmetic: 12.7 us -> none  [the longest x3 7.62 us: shards(): peak = lax.pmax(jnp.max(shifted, axis=1), 'cent')]
  transfers between devices with their start and end apart: 1 -> 0, of which waited for: 1 -> 0; matrix products, arithmetic and copies ran while one was open for 0% -> 0% of each run, Pallas kernels for 0% -> 0%
where the time goes in v2:
time: 143 us; the launch traced here: 142 us
  Pallas kernels  138 us (97%)
  local copies, waits for them, and re-layouts  3.96 us (3%)
    pallas_call x1, Pallas kernels, shards(): pl.pallas_call(functools.partial(kernel, math.log(n_total / k_total), 1.0...  138 us
    unnamed x5, local copies, waits for them, and re-layouts  3.96 us

profile of v2, /device:TPU:6, one launch (start us, length us, event | category | flops | bytes accessed | tf_op | source)
XLA Modules:
  0.0 142.0 jit_solution(3509934112141615610)
XLA Ops:
  0.0 0.0 copy-start
  0.0 1.4 copy-done
  1.4 0.0 copy-start.1
  1.4 1.4 copy-done.1
  2.8 138.0 %balance.1 = bf16[1024,768]{1,0:T(8,128)(2,1)S(1)} custom-call(bf16[1024,768]{1,0:T(8,128)(2,1)S(1)} %copy-done, bf16[1024,768]{1,0:T(8,128)(2,1)S(1)} %copy-done.1), custom_call_target="tpu_custom_call" | custom-call | flops 4831838208 | bytes 4718592 | tf_op jit(solution)/shard_map/balance/pallas_call | solution.py:359
  140.8 1.1 copy.4
Async XLA Ops:
  0.0 1.4 copy-start
  1.4 1.4 copy-start.1

commit v3 on v2

--- a/solution.py
+++ b/solution.py
@@ -38,7 +38,7 @@
     vec, cx, cz, rc, px, mass_out, mass_in, nz,
     in_sem, pts_send, pts_recv, pair_send, pair_recv,
     vec_send, cx_recv, cz_recv, rc_recv, px_recv, mass_send, mass_recv,
-    nz_send, nz_recv, ag_send, agz_recv, agl_recv, agr_recv, agx_recv,
+    nz_send, nz_recv, ag_send, agz_recv, agx_recv,
 ):
     npts, depth = p_ref.shape
     ncent = c_ref.shape[0]
@@ -169,14 +169,26 @@
     swap(vec.at[0], x_peers, cx.at[0], vec_send.at[0], cx_recv.at[0])
 
     mine = aligned(core * half, half)
-    for k in (1, 3, 2):
-        send(p_ref.at[mine], pts.at[k - 1, mine], pts_send, pts_recv.at[k - 1], x_peers[k - 1])
-    pending.append((pts.at[:, mine], pts_send))
-
-    def pass_on(k):
-        landed(pts.at[k - 1, mine], pts_recv.at[k - 1])
-        send(pts.at[k - 1, mine], pts.at[k - 1, mine], pair_send, pair_recv, sibling)
-
+    parts = (aligned(core * half, half // 2), aligned(core * half + half // 2, half // 2))
+
+    def fetch():
+        for k in (1, 3):
+            send(p_ref.at[mine], pts.at[k - 1, mine], pts_send, pts_recv.at[k - 1], x_peers[k - 1])
+
+    def fetch_far():
+        for k, rows in ((1, parts[0]), (3, parts[1])):
+            landed(pts.at[k - 1, mine], pts_recv.at[k - 1])
+            send(pts.at[k - 1, rows], pts.at[1, rows], pts_send, pts_recv.at[1], x_peers[k - 1])
+            send(pts.at[k - 1, mine], pts.at[k - 1, mine], pair_send, pair_recv, sibling)
+
+    def fetch_end():
+        landed(pts.at[1, mine], pts_recv.at[1])
+        send(pts.at[1, mine], pts.at[1, mine], pair_send, pair_recv, sibling)
+        pending.append((pts.at[:, mine], pts_send))
+        pending.append((pts.at[:, mine], pair_send))
+        landed(pts.at[:, aligned(half - core * half, half)], pair_recv)
+
+    fetch()
     landed(cx.at[0], cx_recv.at[0])
     vec[1] = merge(vec[0], cx.at[0], NX - 1)
     swap(vec.at[1], z_peers, cz.at[0], vec_send.at[1], cz_recv.at[0], FAR)
@@ -216,12 +228,9 @@
         vec[at + 1] = add_up(vec[at], cx.at[sweep], NX - 1)
         swap(vec.at[at + 1], z_peers, cz.at[sweep], vec_send.at[at + 1], cz_recv.at[sweep], FAR)
         if sweep == 1:
-            pass_on(1)
-            pass_on(3)
+            fetch_far()
         else:
-            pass_on(2)
-            pending.append((pts.at[:, mine], pair_send))
-            landed(pts.at[:, aligned(half - core * half, half)], pair_recv)
+            fetch_end()
             quarter = c_ref[aligned(x * per_x, per_x), :]
             for k in range(NX):
                 tile[:, k * npts : (k + 1) * npts] = factor * lax.dot_general(
@@ -272,14 +281,14 @@
     def piece(j):
         return num.at[aligned(((z + j) % NZ) * per, per)]
 
+    for t in range(qt):
+        mass_out[t : t + 1, :] = jnp.sum(mass[t * LANES : (t + 1) * LANES, :].T, axis=0, keepdims=True)
+    swap(mass_out, z_peers, mass_in, mass_send, mass_recv, FAR)
     for j in BY_RELAY:
         by = j - 4 if j < 8 else j + 4
         send(piece(j), nz.at[j - 1], nz_send, nz_recv.at[1 if j < 8 else 2], z_peers[by - 1])
     for j in NEAR:
         send(piece(j), nz.at[j - 1], nz_send, nz_recv.at[0], z_peers[j - 1])
-    for t in range(qt):
-        mass_out[t : t + 1, :] = jnp.sum(mass[t * LANES : (t + 1) * LANES, :].T, axis=0, keepdims=True)
-    swap(mass_out, z_peers, mass_in, mass_send, mass_recv, FAR)
     for j, group, slots in ((4, 1, (5, 6, 7)), (12, 2, (8, 9, 10, 11))):
         landed(nz.at[pl.ds(slots[0] - 1, len(slots))], nz_recv.at[group])
         here = piece(j)
@@ -304,27 +313,17 @@
     acc = (acc + c_ref[own, :].astype(f32)) / (mass + 1.0)
     o_ref[own, :] = acc.astype(o_ref.dtype)
 
-    def rows_of(i, j):
-        return o_ref.at[aligned((((x + i) % NX) * NZ + (z + NZ - j) % NZ) * per, per)]
+    def rows_of(j):
+        return o_ref.at[aligned((x * NZ + (z + NZ - j) % NZ) * per, per)]
 
     def hand_on(rows, recv, peer):
         send(rows, rows, ag_send, recv, peer)
 
     for j in (4, 12, 1, 15, 2, 14, 3, 13):
-        hand_on(rows_of(0, 0), agz_recv.at[j], z_peers[j - 1])
-
-    def relay(n):
-        j = LANDING[n]
-        if n % 2:
-            landed(rows_of(1, j), agr_recv.at[j])
-            hand_on(rows_of(1, j), agx_recv, x_peers[2])
-        else:
-            landed(rows_of(3, j), agl_recv.at[j])
-            hand_on(rows_of(3, j), agx_recv, x_peers[0])
-
-    lag = 2
-    for n, j in enumerate(LANDING):
-        rows = rows_of(0, j)
+        hand_on(rows_of(0), agz_recv.at[j], z_peers[j - 1])
+
+    for j in LANDING:
+        rows = rows_of(j)
         if j:
             landed(rows, agz_recv.at[j])
         if j == 4:
@@ -333,13 +332,9 @@
         if j == 12:
             for a in (3, 2, 1):
                 hand_on(rows, agz_recv.at[12 - a], z_peers[NZ - a - 1])
-        hand_on(rows, agx_recv if n % 2 else agl_recv.at[j], x_peers[0])
-        hand_on(rows, agr_recv.at[j] if n % 2 else agx_recv, x_peers[2])
-        if n >= lag:
-            relay(n - lag)
-    for n in range(NZ - lag, NZ):
-        relay(n)
-    landed(o_ref.at[pl.ds(0, 2 * NZ * per)], agx_recv)
+        for peer in (x_peers[1], x_peers[0], x_peers[2]):
+            hand_on(rows, agx_recv, peer)
+    landed(o_ref.at[pl.ds(0, (NX - 1) * per_x)], agx_recv)
     pending.append((o_ref.at[pl.ds(0, (4 * NZ - 1) * per)], ag_send))
 
     drain()
@@ -383,10 +378,10 @@
             pltpu.VMEM((NZ - 1, per, depth), f32),
             dma((5,)), dma, dma((NX - 1,)), dma, dma,
             dma((11,)), dma((3,)), dma((3,)), dma((3,)), dma((2,)), dma, dma,
-            dma, dma((3,)), dma, dma((NZ,)), dma((NZ,)), dma((NZ,)), dma,
+            dma, dma((3,)), dma, dma((NZ,)), dma,
         ],
         compiler_params=pltpu.CompilerParams(
-            collective_id=0, has_side_effects=True, vmem_limit_bytes=48 * 2**20
+            collective_id=0, has_side_effects=True, vmem_limit_bytes=60 * 2**20
         ),
         cost_estimate=pl.CostEstimate(
             flops=6 * npts * ncent * depth, transcendentals=3 * npts * ncent,

time: 143 us -> 123 us (0.86); the launches traced: 142 us -> 120 us
  Pallas kernels: 138 us -> 118 us
    pallas_call x1, Pallas kernels: 138 us -> 118 us  [shards(): pl.pallas_call(functools.partial(kernel, math.log(n_total / k_total), 1.0...]
    unnamed x5 -> x1, local copies, waits for them, and re-layouts: 3.96 us -> 2.65 us
where the time goes in v3:
time: 123 us; the launch traced here: 120 us
  Pallas kernels  118 us (96%)
  local copies, waits for them, and re-layouts  2.65 us (2%)
    pallas_call x1, Pallas kernels, shards(): pl.pallas_call(functools.partial(kernel, math.log(n_total / k_total), 1.0...  118 us
    unnamed x1, local copies, waits for them, and re-layouts  2.65 us

profile of v3, /device:TPU:6, one launch (start us, length us, event | category | flops | bytes accessed | tf_op | source)
XLA Modules:
  0.0 120.4 jit_solution(11187915342799822929)
XLA Ops:
  0.0 117.7 %balance.1 = bf16[1024,768]{1,0:T(8,128)(2,1)} custom-call(bf16[1024,768]{1,0:T(8,128)(2,1)} %p_hbm.1, bf16[1024,768]{1,0:T(8,128)(2,1)} %c_hbm.1), custom_call_target="tpu_custom_call" | custom-call | flops 4831838208 | bytes 4718592 | tf_op jit(solution)/shard_map/balance/pallas_call | solution.py:354
  117.7 2.7 %copy.4 = bf16[1024,768]{1,0:T(8,128)(2,1)} copy(bf16[1024,768]{1,0:T(8,128)(2,1)} %balance.1) | data formatting | bytes 3145728

commit v4 on v3

--- a/solution.py
+++ b/solution.py
@@ -10,6 +10,7 @@
 
 NX, NZ, NC = 4, 16, 8
 LANES = 128
+SPAN = 85.0
 MESH = pl.DeviceIdType.MESH
 FAR = [8, 7, 9, 6, 10, 5, 11, 4, 12, 3, 13, 2, 14, 1, 15]
 NEAR = [3, 13, 2, 14, 1, 15]
@@ -31,13 +32,34 @@
     return jnp.concatenate([rows[t : t + 1, :] for t in range(tiles)], axis=1)
 
 
+def coded(value, mass):
+    most = jnp.max(jnp.abs(value), axis=1, keepdims=True)
+    scale = jnp.maximum(most * 1.01, 1e-30).astype(jnp.bfloat16).astype(jnp.float32)
+    power = jnp.exp(jnp.abs(value) * (2.0 * SPAN / scale) - SPAN)
+    power = jnp.where(value < 0.0, -power, power)
+    high = mass.astype(jnp.bfloat16).astype(jnp.float32)
+    middle = (mass - high).astype(jnp.bfloat16).astype(jnp.float32)
+    lane = lax.broadcasted_iota(jnp.int32, (value.shape[0], LANES), 1)
+    more = jnp.where(lane == 0, scale, jnp.where(lane == 1, high, jnp.where(lane == 2, middle, mass - high - middle)))
+    return jnp.concatenate([power, more], axis=1).astype(jnp.bfloat16)
+
+
+def decoded(piece):
+    depth = piece.shape[1] - LANES
+    power = piece[:, :depth].astype(jnp.float32)
+    more = piece[:, depth:].astype(jnp.float32)
+    value = (jnp.log(jnp.abs(power)) + SPAN) * (more[:, :1] * (0.5 / SPAN))
+    mass = more[:, 1:2] + more[:, 2:3] + more[:, 3:4]
+    return jnp.where(power < 0.0, -value, value), mass
+
+
 def kernel(
     log_mass, factor,
     p_hbm, c_hbm, o_ref,
-    p_ref, c_ref, pts, mat, scale, tile, num, total, part, top, cpot,
-    vec, cx, cz, rc, px, mass_out, mass_in, nz,
+    p_ref, c_ref, pts, mat, scale, tile, num, masses, total, part, top, cpot,
+    vec, cx, cz, rc, px, code, nz,
     in_sem, pts_send, pts_recv, pair_send, pair_recv,
-    vec_send, cx_recv, cz_recv, rc_recv, px_recv, mass_send, mass_recv,
+    vec_send, cx_recv, cz_recv, rc_recv, px_recv,
     nz_send, nz_recv, ag_send, agz_recv, agx_recv,
 ):
     npts, depth = p_ref.shape
@@ -279,36 +301,35 @@
     num[...] = acc
 
     def piece(j):
-        return num.at[aligned(((z + j) % NZ) * per, per)]
-
-    for t in range(qt):
-        mass_out[t : t + 1, :] = jnp.sum(mass[t * LANES : (t + 1) * LANES, :].T, axis=0, keepdims=True)
-    swap(mass_out, z_peers, mass_in, mass_send, mass_recv, FAR)
+        return aligned(((z + j) % NZ) * per, per)
+
+    def send_piece(j, by, at):
+        send(code.at[piece(j)], nz.at[j - 1], nz_send, nz_recv.at[at], z_peers[by - 1])
+
+    def gathered(j, slots):
+        rows = piece(j)
+        acc, held = num[rows, :], masses[rows, :][:, :1]
+        for i in slots:
+            value, mass = decoded(nz[i - 1])
+            acc += value
+            held += mass
+        return acc, held
+
+    mass = jnp.sum(mass, axis=1, keepdims=True)
+    masses[...] = jnp.broadcast_to(mass, masses.shape)
+    code[...] = coded(acc, mass)
     for j in BY_RELAY:
-        by = j - 4 if j < 8 else j + 4
-        send(piece(j), nz.at[j - 1], nz_send, nz_recv.at[1 if j < 8 else 2], z_peers[by - 1])
+        send_piece(j, j - 4 if j < 8 else j + 4, 1 if j < 8 else 2)
     for j in NEAR:
-        send(piece(j), nz.at[j - 1], nz_send, nz_recv.at[0], z_peers[j - 1])
-    for j, group, slots in ((4, 1, (5, 6, 7)), (12, 2, (8, 9, 10, 11))):
-        landed(nz.at[pl.ds(slots[0] - 1, len(slots))], nz_recv.at[group])
-        here = piece(j)
-        acc = here[...]
-        for i in slots:
-            acc += nz[i - 1]
-        here[...] = acc
-        send(here, nz.at[j - 1], nz_send, nz_recv.at[0], z_peers[j - 1])
+        send_piece(j, j, 0)
+    for j, at, slots in ((4, 1, (5, 6, 7)), (12, 2, (8, 9, 10, 11))):
+        landed(nz.at[pl.ds(slots[0] - 1, len(slots))], nz_recv.at[at])
+        code[piece(j), :] = coded(*gathered(j, slots))
+        send_piece(j, j, 0)
     pending.append((nz, nz_send))
 
-    landed(mass_in, mass_recv)
-    total[:qt, :] = add_up(mass_out[...], mass_in, NZ - 1)
-    row = total[pl.ds(z * per // LANES, 1), :]
-    scale[:LANES, :] = jnp.broadcast_to(row, (LANES, LANES)).T
-    mass = scale[aligned((z * per) % LANES, per), :][:, :1]
-
     landed(nz.at[pl.ds(0, 8)], nz_recv.at[0])
-    acc = piece(0)[...]
-    for j in NEAR + [4, 12]:
-        acc += nz[j - 1]
+    acc, mass = gathered(0, NEAR + [4, 12])
     own = aligned((x * NZ + z) * per, per)
     acc = (acc + c_ref[own, :].astype(f32)) / (mass + 1.0)
     o_ref[own, :] = acc.astype(o_ref.dtype)
@@ -364,6 +385,7 @@
             pltpu.VMEM((npts, LANES), f32),
             pltpu.VMEM((per_x, NX * npts), f32),
             pltpu.VMEM((per_x, depth), f32),
+            pltpu.VMEM((per_x, LANES), f32),
             pltpu.VMEM((ct, LANES), f32),
             pltpu.VMEM((rt, LANES), f32),
             pltpu.VMEM((rt, LANES), f32),
@@ -373,11 +395,10 @@
             pltpu.VMEM((3, NZ - 1, ct, LANES), f32),
             pltpu.VMEM((3, NC - 1, rt, LANES), f32),
             pltpu.VMEM((2, NX - 1, rt, LANES), f32),
-            pltpu.VMEM((per_x // LANES, LANES), f32),
-            pltpu.VMEM((NZ - 1, per_x // LANES, LANES), f32),
-            pltpu.VMEM((NZ - 1, per, depth), f32),
+            pltpu.VMEM((per_x, depth + LANES), bf16),
+            pltpu.VMEM((NZ - 1, per, depth + LANES), bf16),
             dma((5,)), dma, dma((NX - 1,)), dma, dma,
-            dma((11,)), dma((3,)), dma((3,)), dma((3,)), dma((2,)), dma, dma,
+            dma((11,)), dma((3,)), dma((3,)), dma((3,)), dma((2,)),
             dma, dma((3,)), dma, dma((NZ,)), dma,
         ],
         compiler_params=pltpu.CompilerParams(

time: 123 us -> 112 us (0.911); the launches traced: 120 us -> 111 us
  Pallas kernels: 118 us -> 108 us
    pallas_call x1, Pallas kernels: 118 us -> 108 us  [shards(): pl.pallas_call(functools.partial(kernel, math.log(n_total / k_total), 1.0...]
where the time goes in v4:
time: 112 us; the launch traced here: 111 us
  Pallas kernels  108 us (96%)
  local copies, waits for them, and re-layouts  2.65 us (2%)
    pallas_call x1, Pallas kernels, shards(): pl.pallas_call(functools.partial(kernel, math.log(n_total / k_total), 1.0...  108 us
    unnamed x1, local copies, waits for them, and re-layouts  2.65 us

profile of v4, /device:TPU:6, one launch (start us, length us, event | category | flops | bytes accessed | tf_op | source)
XLA Modules:
  0.0 110.9 jit_solution(11857452174617196820)
XLA Ops:
  0.0 108.3 %balance.1 = bf16[1024,768]{1,0:T(8,128)(2,1)} custom-call(bf16[1024,768]{1,0:T(8,128)(2,1)} %p_hbm.1, bf16[1024,768]{1,0:T(8,128)(2,1)} %c_hbm.1), custom_call_target="tpu_custom_call" | custom-call | flops 4831838208 | bytes 4718592 | tf_op jit(solution)/shard_map/balance/pallas_call | solution.py:375
  108.3 2.7 %copy.4 = bf16[1024,768]{1,0:T(8,128)(2,1)} copy(bf16[1024,768]{1,0:T(8,128)(2,1)} %balance.1) | data formatting | bytes 3145728

commit v5 on v4

--- a/solution.py
+++ b/solution.py
@@ -15,7 +15,7 @@
 FAR = [8, 7, 9, 6, 10, 5, 11, 4, 12, 3, 13, 2, 14, 1, 15]
 NEAR = [3, 13, 2, 14, 1, 15]
 BY_RELAY = [8, 9, 7, 10, 6, 11, 5]
-LANDING = [0, 4, 12, 1, 15, 2, 14, 3, 13, 5, 11, 6, 10, 7, 9, 8]
+LANDING = [0, 4, 12, 3, 13, 2, 14, 1, 15, 5, 11, 6, 10, 7, 9, 8]
 
 
 def aligned(start, size):
@@ -152,7 +152,7 @@
             return tuple(out)
 
         zero = tuple(jnp.zeros((8, LANES), f32) for _ in range(ct))
-        acc = lax.fori_loop(0, rt, step, zero)
+        acc = lax.fori_loop(0, rt, step, zero, unroll=True)
         return jnp.concatenate([jnp.sum(a, axis=0, keepdims=True) for a in acc], axis=0)
 
     def row_sums(wide):
@@ -164,7 +164,7 @@
             part[pl.ds(r, 1), :] = jnp.sum(acc.T, axis=0, keepdims=True)
             return carry
 
-        lax.fori_loop(0, rt, step, 0)
+        lax.fori_loop(0, rt, step, 0, unroll=True)
 
     c_in.wait()
     peak8 = jnp.full((8, ncent), -jnp.inf, f32)
@@ -183,7 +183,7 @@
         got = jnp.exp(mat[rows, :] - peak)
         return acc + jnp.sum(got.reshape(LANES // 8, 8, ncent), axis=0)
 
-    acc = lax.fori_loop(0, rt, first_sum, jnp.zeros((8, ncent), f32))
+    acc = lax.fori_loop(0, rt, first_sum, jnp.zeros((8, ncent), f32), unroll=True)
     vec[0] = to_rows(peak + jnp.log(jnp.sum(acc, axis=0, keepdims=True)), ct)
 
     pl.semaphore_wait(barrier, NX + NZ + NC - 3)
@@ -234,7 +234,7 @@
         top[pl.ds(r, 1), :] = jnp.broadcast_to(high, (LANES, LANES)).T[:1, :]
         return carry
 
-    lax.fori_loop(0, rt, first_rows, 0)
+    lax.fori_loop(0, rt, first_rows, 0, unroll=True)
     vec[2] = top[...] + jnp.log(part[...])
     swap(vec.at[2], c_peers, rc.at[0], vec_send.at[2], rc_recv.at[0])
     landed(rc.at[0], rc_recv.at[0])
@@ -340,7 +340,7 @@
     def hand_on(rows, recv, peer):
         send(rows, rows, ag_send, recv, peer)
 
-    for j in (4, 12, 1, 15, 2, 14, 3, 13):
+    for j in (4, 12, 3, 13, 2, 14, 1, 15):
         hand_on(rows_of(0), agz_recv.at[j], z_peers[j - 1])
 
     for j in LANDING:
@@ -402,7 +402,7 @@
             dma, dma((3,)), dma, dma((NZ,)), dma,
         ],
         compiler_params=pltpu.CompilerParams(
-            collective_id=0, has_side_effects=True, vmem_limit_bytes=60 * 2**20
+            collective_id=0, has_side_effects=True, vmem_limit_bytes=52 * 2**20
         ),
         cost_estimate=pl.CostEstimate(
             flops=6 * npts * ncent * depth, transcendentals=3 * npts * ncent,

time: 112 us -> 106 us (0.946)
  Pallas kernels: 108 us -> 104 us
  local copies, waits for them, and re-layouts: 2.65 us -> 1.15 us
    pallas_call x1, Pallas kernels: 108 us -> 104 us  [shards(): pl.pallas_call(functools.partial(kernel, math.log(n_total / k_total), 1.0...]
    unnamed x1, local copies, waits for them, and re-layouts: 2.65 us -> 1.15 us
where the time goes in v5:
time: 106 us; the launch traced here: 105 us
  Pallas kernels  104 us (98%)
  local copies, waits for them, and re-layouts  1.15 us (1%)
    pallas_call x1, Pallas kernels, shards(): pl.pallas_call(functools.partial(kernel, math.log(n_total / k_total), 1.0...  104 us

profile of v5, /device:TPU:6, one launch (start us, length us, event | category | flops | bytes accessed | tf_op | source)
XLA Modules:
  0.0 105.0 jit_solution(3096099885558771983)
XLA Ops:
  0.0 103.9 %balance.1 = bf16[1024,768]{1,0:T(8,128)(2,1)S(1)} custom-call(bf16[1024,768]{1,0:T(8,128)(2,1)} %p_hbm.1, bf16[1024,768]{1,0:T(8,128)(2,1)} %c_hbm.1), custom_call_target="tpu_custom_call" | custom-call | flops 4831838208 | bytes 4718592 | tf_op jit(solution)/shard_map/balance/pallas_call | solution.py:375
  103.9 1.1 %copy.4 = bf16[1024,768]{1,0:T(8,128)(2,1)} copy(bf16[1024,768]{1,0:T(8,128)(2,1)S(1)} %balance.1) | data formatting | bytes 3145728

commit v6 on v5

--- a/solution.py
+++ b/solution.py
@@ -13,9 +13,19 @@
 SPAN = 85.0
 MESH = pl.DeviceIdType.MESH
 FAR = [8, 7, 9, 6, 10, 5, 11, 4, 12, 3, 13, 2, 14, 1, 15]
+FAR_C = [4, 3, 5, 2, 6, 1, 7]
+FAR_X = [2, 1, 3]
 NEAR = [3, 13, 2, 14, 1, 15]
-BY_RELAY = [8, 9, 7, 10, 6, 11, 5]
-LANDING = [0, 4, 12, 3, 13, 2, 14, 1, 15, 5, 11, 6, 10, 7, 9, 8]
+BY_RELAY = [9, 7, 10, 6, 11, 5]
+LAG, RINGED = 8, 22
+LANDING = (
+    [(0, 0), (1, 0)]
+    + [(0, j) for j in (4, 12, 3, 13)]
+    + [(1, j) for j in (4, 12)]
+    + [(0, j) for j in (2, 14, 1, 15)]
+    + [(1, j) for j in (3, 13, 2, 14, 1, 15)]
+    + [(h, j) for h in (0, 1) for j in (5, 11, 6, 10, 7, 9, 8)]
+)
 
 
 def aligned(start, size):
@@ -32,35 +42,37 @@
     return jnp.concatenate([rows[t : t + 1, :] for t in range(tiles)], axis=1)
 
 
-def coded(value, mass):
-    most = jnp.max(jnp.abs(value), axis=1, keepdims=True)
-    scale = jnp.maximum(most * 1.01, 1e-30).astype(jnp.bfloat16).astype(jnp.float32)
+def coded(value, scale):
     power = jnp.exp(jnp.abs(value) * (2.0 * SPAN / scale) - SPAN)
-    power = jnp.where(value < 0.0, -power, power)
+    return jnp.where(value < 0.0, -power, power).astype(jnp.bfloat16)
+
+
+def decoded(power, scale):
+    power = power.astype(jnp.float32)
+    value = (jnp.log(jnp.abs(power)) + SPAN) * (scale * (0.5 / SPAN))
+    return jnp.where(power < 0.0, -value, value)
+
+
+def scale_of(most):
+    return jnp.maximum(most * 1.01, 1e-30).astype(jnp.bfloat16).astype(jnp.float32)
+
+
+def further(scale, mass):
     high = mass.astype(jnp.bfloat16).astype(jnp.float32)
     middle = (mass - high).astype(jnp.bfloat16).astype(jnp.float32)
-    lane = lax.broadcasted_iota(jnp.int32, (value.shape[0], LANES), 1)
+    lane = lax.broadcasted_iota(jnp.int32, (mass.shape[0], LANES), 1)
     more = jnp.where(lane == 0, scale, jnp.where(lane == 1, high, jnp.where(lane == 2, middle, mass - high - middle)))
-    return jnp.concatenate([power, more], axis=1).astype(jnp.bfloat16)
-
-
-def decoded(piece):
-    depth = piece.shape[1] - LANES
-    power = piece[:, :depth].astype(jnp.float32)
-    more = piece[:, depth:].astype(jnp.float32)
-    value = (jnp.log(jnp.abs(power)) + SPAN) * (more[:, :1] * (0.5 / SPAN))
-    mass = more[:, 1:2] + more[:, 2:3] + more[:, 3:4]
-    return jnp.where(power < 0.0, -value, value), mass
+    return more.astype(jnp.bfloat16)
 
 
 def kernel(
     log_mass, factor,
     p_hbm, c_hbm, o_ref,
-    p_ref, c_ref, pts, mat, scale, tile, num, masses, total, part, top, cpot,
-    vec, cx, cz, rc, px, code, nz,
+    p_ref, c_ref, pts, mat, scale, tile, num, masses, scales, total, part, top, cpot,
+    vec, cx, cz, rc, px, code_a, code_b, nz_a, nz_b,
     in_sem, pts_send, pts_recv, pair_send, pair_recv,
     vec_send, cx_recv, cz_recv, rc_recv, px_recv,
-    nz_send, nz_recv, ag_send, agz_recv, agx_recv,
+    nz_send, nz_recv, ag_send, agz_recv, agx_recv, agn_recv,
 ):
     npts, depth = p_ref.shape
     ncent = c_ref.shape[0]
@@ -102,6 +114,9 @@
         pl.semaphore_signal(barrier, inc=1, device_id=peer, device_id_type=MESH)
 
     pending = []
+
+    def on_core(which, go):
+        pl.when(core == which)(go)
 
     def send(src, dst, send_sem, recv_sem, peer):
         pltpu.make_async_remote_copy(
@@ -188,7 +203,7 @@
 
     pl.semaphore_wait(barrier, NX + NZ + NC - 3)
 
-    swap(vec.at[0], x_peers, cx.at[0], vec_send.at[0], cx_recv.at[0])
+    swap(vec.at[0], x_peers, cx.at[0], vec_send.at[0], cx_recv.at[0], FAR_X)
 
     mine = aligned(core * half, half)
     parts = (aligned(core * half, half // 2), aligned(core * half + half // 2, half // 2))
@@ -236,7 +251,7 @@
 
     lax.fori_loop(0, rt, first_rows, 0, unroll=True)
     vec[2] = top[...] + jnp.log(part[...])
-    swap(vec.at[2], c_peers, rc.at[0], vec_send.at[2], rc_recv.at[0])
+    swap(vec.at[2], c_peers, rc.at[0], vec_send.at[2], rc_recv.at[0], FAR_C)
     landed(rc.at[0], rc_recv.at[0])
     row_pot = -merge(vec[2], rc.at[0], NC - 1)
     u = jnp.exp(top[...] + row_pot)
@@ -245,7 +260,7 @@
     for sweep in (1, 2):
         at = 3 * sweep
         vec[at] = column_sums()
-        swap(vec.at[at], x_peers, cx.at[sweep], vec_send.at[at], cx_recv.at[sweep])
+        swap(vec.at[at], x_peers, cx.at[sweep], vec_send.at[at], cx_recv.at[sweep], FAR_X)
         landed(cx.at[sweep], cx_recv.at[sweep])
         vec[at + 1] = add_up(vec[at], cx.at[sweep], NX - 1)
         swap(vec.at[at + 1], z_peers, cz.at[sweep], vec_send.at[at + 1], cz_recv.at[sweep], FAR)
@@ -264,7 +279,7 @@
         v = math.exp(log_mass) / add_up(vec[at + 1], cz.at[sweep], NZ - 1)
         row_sums(to_wide(v, ct))
         vec[at + 2] = u * part[...]
-        swap(vec.at[at + 2], c_peers, rc.at[sweep], vec_send.at[at + 2], rc_recv.at[sweep])
+        swap(vec.at[at + 2], c_peers, rc.at[sweep], vec_send.at[at + 2], rc_recv.at[sweep], FAR_C)
         if sweep == 2:
             total[...] = col_pot + jnp.log(v)
             spread(total[pl.ds(x * qt, qt), :], cpot, qt)
@@ -282,7 +297,7 @@
             spread(u, scale, rt)
         else:
             vec[10] = 1.0 / got
-            swap(vec.at[10], x_peers, px.at[1], vec_send.at[10], px_recv.at[1])
+            swap(vec.at[10], x_peers, px.at[1], vec_send.at[10], px_recv.at[1], FAR_X)
             landed(px.at[1], px_recv.at[1])
 
     mass = jnp.zeros((per_x, LANES), f32)
@@ -300,62 +315,125 @@
         )
     num[...] = acc
 
+    width = depth // 2
+    codes, lands = (code_a, code_b), (nz_a, nz_b)
+
+    def columns(h):
+        return slice(h * width, (h + 1) * width)
+
     def piece(j):
         return aligned(((z + j) % NZ) * per, per)
 
-    def send_piece(j, by, at):
-        send(code.at[piece(j)], nz.at[j - 1], nz_send, nz_recv.at[at], z_peers[by - 1])
-
-    def gathered(j, slots):
-        rows = piece(j)
-        acc, held = num[rows, :], masses[rows, :][:, :1]
+    def send_piece(h, j, by, at):
+        send(codes[h].at[piece(j)], lands[h].at[j - 1], nz_send.at[h], nz_recv.at[h, at], z_peers[by - 1])
+
+    def scale_in(i):
+        return nz_a[i - 1, :, width : width + 1].astype(f32)
+
+    def gathered(h, j, slots):
+        acc = num[piece(j), columns(h)]
         for i in slots:
-            value, mass = decoded(nz[i - 1])
-            acc += value
-            held += mass
-        return acc, held
+            acc += decoded(lands[h][i - 1, :, :width], scale_in(i))
+        return acc
+
+    def gathered_mass(j, slots):
+        held = masses[piece(j), :][:, :1]
+        for i in slots:
+            held += mass_in(i)
+        return held
+
+    def mass_in(i):
+        more = nz_a[i - 1, :, width:].astype(f32)
+        return more[:, 1:2] + more[:, 2:3] + more[:, 3:4]
 
     mass = jnp.sum(mass, axis=1, keepdims=True)
     masses[...] = jnp.broadcast_to(mass, masses.shape)
-    code[...] = coded(acc, mass)
-    for j in BY_RELAY:
-        send_piece(j, j - 4 if j < 8 else j + 4, 1 if j < 8 else 2)
-    for j in NEAR:
-        send_piece(j, j, 0)
-    for j, at, slots in ((4, 1, (5, 6, 7)), (12, 2, (8, 9, 10, 11))):
-        landed(nz.at[pl.ds(slots[0] - 1, len(slots))], nz_recv.at[at])
-        code[piece(j), :] = coded(*gathered(j, slots))
-        send_piece(j, j, 0)
-    pending.append((nz, nz_send))
-
-    landed(nz.at[pl.ds(0, 8)], nz_recv.at[0])
-    acc, mass = gathered(0, NEAR + [4, 12])
-    own = aligned((x * NZ + z) * per, per)
-    acc = (acc + c_ref[own, :].astype(f32)) / (mass + 1.0)
-    o_ref[own, :] = acc.astype(o_ref.dtype)
-
-    def rows_of(j):
-        return o_ref.at[aligned((x * NZ + (z + NZ - j) % NZ) * per, per)]
+    row_scale = scale_of(jnp.max(jnp.abs(acc), axis=1, keepdims=True))
+    scales[...] = jnp.broadcast_to(row_scale, scales.shape)
+    code_a[:, :width] = coded(acc[:, :width], row_scale)
+    code_a[:, width:] = further(row_scale, mass)
+
+    def send_far(h):
+        on_core(0, lambda: send_piece(h, 8, 12, 3))
+        on_core(1, lambda: send_piece(h, 8, 4, 3))
+        for j in BY_RELAY:
+            send_piece(h, j, j - 4 if j < 8 else j + 4, 1 if j < 8 else 2)
+
+    send_far(0)
+    code_b[...] = coded(acc[:, width:], row_scale)
+    send_far(1)
+    for h in range(2):
+        for j in NEAR:
+            send_piece(h, j, j, 0)
+        landed(lands[h].at[7], nz_recv.at[h, 3])
+        for j, at, slots in ((4, 1, (5, 6, 7)), (12, 2, (9, 10, 11))):
+            far = (core == (1 if j == 4 else 0)).astype(f32)
+            landed(lands[h].at[pl.ds(slots[0] - 1, len(slots))], nz_recv.at[h, at])
+            if h == 0:
+                most = scales[piece(j), :][:, :1] + far * scale_in(8)
+                for i in slots:
+                    most += scale_in(i)
+                most = scale_of(most)
+                scales[piece(j), :] = jnp.broadcast_to(most, (per, LANES))
+                code_a[piece(j), width:] = further(most, gathered_mass(j, slots) + far * mass_in(8))
+            codes[h][piece(j), :width] = coded(
+                gathered(h, j, slots) + far * decoded(lands[h][7, :, :width], scale_in(8)), scales[piece(j), :][:, :1]
+            )
+            send_piece(h, j, j, 0)
+        pending.append((lands[h], nz_send.at[h]))
+
+    def rows_of(h, j):
+        return o_ref.at[aligned((x * NZ + (z + NZ - j) % NZ) * per, per), pl.ds(h * width, width)]
 
     def hand_on(rows, recv, peer):
         send(rows, rows, ag_send, recv, peer)
 
-    for j in (4, 12, 3, 13, 2, 14, 1, 15):
-        hand_on(rows_of(0), agz_recv.at[j], z_peers[j - 1])
-
-    for j in LANDING:
-        rows = rows_of(j)
-        if j:
-            landed(rows, agz_recv.at[j])
+    def rows_x(n, i):
+        h, j = LANDING[n]
+        return o_ref.at[
+            aligned((((x + i) % NX) * NZ + (z + NZ - j) % NZ) * per, per), pl.ds(h * width, width)
+        ]
+
+    def hand_x(n):
+        rows = rows_x(n, 0)
+        if n >= RINGED:
+            hand_on(rows, agx_recv, x_peers[1])
+        hand_on(rows, agx_recv if n % 2 or n >= RINGED else agn_recv.at[n], x_peers[0])
+        hand_on(rows, agn_recv.at[n] if n % 2 and n < RINGED else agx_recv, x_peers[2])
+
+    def relay_x(n):
+        rows = rows_x(n, 1 if n % 2 else 3)
+        landed(rows, agn_recv.at[n])
+        hand_on(rows, agx_recv, x_peers[2 if n % 2 else 0])
+
+    own = aligned((x * NZ + z) * per, per)
+    ends = NEAR + [4, 12]
+    for h in range(2):
+        landed(lands[h].at[pl.ds(0, 8)], nz_recv.at[h, 0])
+        if h == 0:
+            mass = gathered_mass(0, ends)
+        acc = (gathered(h, 0, ends) + c_ref[own, columns(h)].astype(f32)) / (mass + 1.0)
+        o_ref[own, columns(h)] = acc.astype(o_ref.dtype)
+        for j in (4, 12, 3, 13, 2, 14, 1, 15):
+            hand_on(rows_of(h, 0), agz_recv.at[h, j], z_peers[j - 1])
+        hand_x(h)
+
+    for n in range(2, 2 * NZ):
+        h, j = LANDING[n]
+        rows = rows_of(h, j)
+        landed(rows, agz_recv.at[h, j])
         if j == 4:
-            for a in (4, 3, 2, 1):
-                hand_on(rows, agz_recv.at[4 + a], z_peers[a - 1])
+            on_core(0, lambda: hand_on(rows, agz_recv.at[h, 8], z_peers[3]))
+            for a in (3, 2, 1):
+                hand_on(rows, agz_recv.at[h, 4 + a], z_peers[a - 1])
         if j == 12:
+            on_core(1, lambda: hand_on(rows, agz_recv.at[h, 8], z_peers[NZ - 5]))
             for a in (3, 2, 1):
-                hand_on(rows, agz_recv.at[12 - a], z_peers[NZ - a - 1])
-        for peer in (x_peers[1], x_peers[0], x_peers[2]):
-            hand_on(rows, agx_recv, peer)
-    landed(o_ref.at[pl.ds(0, (NX - 1) * per_x)], agx_recv)
+                hand_on(rows, agz_recv.at[h, 12 - a], z_peers[NZ - a - 1])
+        hand_x(n)
+        if LAG <= n < LAG + RINGED:
+            relay_x(n - LAG)
+    landed(o_ref.at[pl.ds(0, (NX - 1) * per_x - RINGED * per // 2)], agx_recv)
     pending.append((o_ref.at[pl.ds(0, (4 * NZ - 1) * per)], ag_send))
 
     drain()
@@ -386,6 +464,7 @@
             pltpu.VMEM((per_x, NX * npts), f32),
             pltpu.VMEM((per_x, depth), f32),
             pltpu.VMEM((per_x, LANES), f32),
+            pltpu.VMEM((per_x, LANES), f32),
             pltpu.VMEM((ct, LANES), f32),
             pltpu.VMEM((rt, LANES), f32),
             pltpu.VMEM((rt, LANES), f32),
@@ -395,11 +474,13 @@
             pltpu.VMEM((3, NZ - 1, ct, LANES), f32),
             pltpu.VMEM((3, NC - 1, rt, LANES), f32),
             pltpu.VMEM((2, NX - 1, rt, LANES), f32),
-            pltpu.VMEM((per_x, depth + LANES), bf16),
-            pltpu.VMEM((NZ - 1, per, depth + LANES), bf16),
+            pltpu.VMEM((per_x, depth // 2 + LANES), bf16),
+            pltpu.VMEM((per_x, depth // 2), bf16),
+            pltpu.VMEM((NZ - 1, per, depth // 2 + LANES), bf16),
+            pltpu.VMEM((NZ - 1, per, depth // 2), bf16),
             dma((5,)), dma, dma((NX - 1,)), dma, dma,
             dma((11,)), dma((3,)), dma((3,)), dma((3,)), dma((2,)),
-            dma, dma((3,)), dma, dma((NZ,)), dma,
+            dma((2,)), dma((2, 4)), dma, dma((2, NZ)), dma, dma((2 * NZ,)),
         ],
         compiler_params=pltpu.CompilerParams(
             collective_id=0, has_side_effects=True, vmem_limit_bytes=52 * 2**20

time: 106 us -> 103 us (0.972)
  Pallas kernels: 104 us -> 101 us
    pallas_call x1, Pallas kernels: 104 us -> 101 us  [shards(): pl.pallas_call(functools.partial(kernel, math.log(n_total / k_total), 1.0...]
where the time goes in v6:
time: 103 us; the launch traced here: 102 us
  Pallas kernels  101 us (98%)
  local copies, waits for them, and re-layouts  1.15 us (1%)
    pallas_call x1, Pallas kernels, shards(): pl.pallas_call(functools.partial(kernel, math.log(n_total / k_total), 1.0...  101 us

profile of v6, /device:TPU:6, one launch (start us, length us, event | category | flops | bytes accessed | tf_op | source)
XLA Modules:
  0.0 101.9 jit_solution(6751390298084795550)
XLA Ops:
  0.0 100.7 %balance.1 = bf16[1024,768]{1,0:T(8,128)(2,1)S(1)} custom-call(bf16[1024,768]{1,0:T(8,128)(2,1)} %p_hbm.1, bf16[1024,768]{1,0:T(8,128)(2,1)} %c_hbm.1), custom_call_target="tpu_custom_call" | custom-call | flops 4831838208 | bytes 4718592 | tf_op jit(solution)/shard_map/balance/pallas_call | solution.py:453
  100.7 1.1 %copy.4 = bf16[1024,768]{1,0:T(8,128)(2,1)} copy(bf16[1024,768]{1,0:T(8,128)(2,1)S(1)} %balance.1) | data formatting | bytes 3145728

commit v7 on v6

--- a/solution.py
+++ b/solution.py
@@ -15,16 +15,17 @@
 FAR = [8, 7, 9, 6, 10, 5, 11, 4, 12, 3, 13, 2, 14, 1, 15]
 FAR_C = [4, 3, 5, 2, 6, 1, 7]
 FAR_X = [2, 1, 3]
+FAR_BOTH = [k * NC + m for k in FAR_X for m in FAR_C] + [k * NC for k in FAR_X] + FAR_C
 NEAR = [3, 13, 2, 14, 1, 15]
 BY_RELAY = [9, 7, 10, 6, 11, 5]
-LAG, RINGED = 8, 22
+LAG, RINGED = 12, 20
 LANDING = (
     [(0, 0), (1, 0)]
     + [(0, j) for j in (4, 12, 3, 13)]
     + [(1, j) for j in (4, 12)]
     + [(0, j) for j in (2, 14, 1, 15)]
     + [(1, j) for j in (3, 13, 2, 14, 1, 15)]
-    + [(h, j) for h in (0, 1) for j in (5, 11, 6, 10, 7, 9, 8)]
+    + [(h, j) for h in (0, 1) for j in (6, 10, 5, 11, 7, 9, 8)]
 )
 
 
@@ -69,7 +70,7 @@
     log_mass, factor,
     p_hbm, c_hbm, o_ref,
     p_ref, c_ref, pts, mat, scale, tile, num, masses, scales, total, part, top, cpot,
-    vec, cx, cz, rc, px, code_a, code_b, nz_a, nz_b,
+    vec, cx, cz, rc, rb, px, inverse, code_a, code_b, nz_a, nz_b,
     in_sem, pts_send, pts_recv, pair_send, pair_recv,
     vec_send, cx_recv, cz_recv, rc_recv, px_recv,
     nz_send, nz_recv, ag_send, agz_recv, agx_recv, agn_recv,
@@ -100,6 +101,11 @@
     x_peers = [x_peer(k) for k in range(1, NX)]
     z_peers = [z_peer(k) for k in range(1, NZ)]
     c_peers = [c_peer(k) for k in range(1, NC)]
+    both = [{**x_peer(k), **c_peer(m)} for k in range(NX) for m in range(NC)][1:]
+
+    barrier = pltpu.get_barrier_semaphore()
+    for peer in [z_peers[j - 1] for j in FAR] + both:
+        pl.semaphore_signal(barrier, inc=1, device_id=peer, device_id_type=MESH)
 
     c_in = pltpu.make_async_copy(c_hbm, c_ref, in_sem.at[4])
     c_in.start()
@@ -108,10 +114,6 @@
         rows = pl.ds(r * (npts // 4), npts // 4)
         p_in.append(pltpu.make_async_copy(p_hbm.at[rows], p_ref.at[rows], in_sem.at[r]))
         p_in[-1].start()
-
-    barrier = pltpu.get_barrier_semaphore()
-    for peer in x_peers + z_peers + c_peers:
-        pl.semaphore_signal(barrier, inc=1, device_id=peer, device_id_type=MESH)
 
     pending = []
 
@@ -201,7 +203,7 @@
     acc = lax.fori_loop(0, rt, first_sum, jnp.zeros((8, ncent), f32), unroll=True)
     vec[0] = to_rows(peak + jnp.log(jnp.sum(acc, axis=0, keepdims=True)), ct)
 
-    pl.semaphore_wait(barrier, NX + NZ + NC - 3)
+    pl.semaphore_wait(barrier, NX * NC + NZ - 2)
 
     swap(vec.at[0], x_peers, cx.at[0], vec_send.at[0], cx_recv.at[0], FAR_X)
 
@@ -274,36 +276,42 @@
                     quarter, p_ref[...] if k == 0 else pts[k - 1],
                     (((1,), (1,)), ((), ())), preferred_element_type=f32,
                 )
-            landed(px.at[0], px_recv.at[0])
+            landed(px, px_recv)
         landed(cz.at[sweep], cz_recv.at[sweep])
         v = math.exp(log_mass) / add_up(vec[at + 1], cz.at[sweep], NZ - 1)
         row_sums(to_wide(v, ct))
         vec[at + 2] = u * part[...]
-        swap(vec.at[at + 2], c_peers, rc.at[sweep], vec_send.at[at + 2], rc_recv.at[sweep], FAR_C)
+        if sweep == 1:
+            swap(vec.at[at + 2], c_peers, rc.at[sweep], vec_send.at[at + 2], rc_recv.at[sweep], FAR_C)
+        else:
+            swap(vec.at[at + 2], both, rb, vec_send.at[at + 2], rc_recv.at[sweep], FAR_BOTH)
         if sweep == 2:
             total[...] = col_pot + jnp.log(v)
             spread(total[pl.ds(x * qt, qt), :], cpot, qt)
             for k in range(NX):
-                pot = vec[9] if k == 0 else px[0, k - 1]
+                pot = vec[9] if k == 0 else px[k - 1]
                 for t in range(rt):
                     cols = slice(k * npts + t * LANES, k * npts + (t + 1) * LANES)
                     tile[:, cols] = jnp.exp(tile[:, cols] + (cpot[...] + pot[t : t + 1, :]))
-        landed(rc.at[sweep], rc_recv.at[sweep])
-        got = add_up(vec[at + 2], rc.at[sweep], NC - 1)
         if sweep == 1:
+            landed(rc.at[sweep], rc_recv.at[sweep])
+            got = add_up(vec[at + 2], rc.at[sweep], NC - 1)
             u = u / got
             vec[9] = row_pot - jnp.log(got)
-            swap(vec.at[9], x_peers, px.at[0], vec_send.at[9], px_recv.at[0])
+            swap(vec.at[9], x_peers, px, vec_send.at[9], px_recv)
             spread(u, scale, rt)
         else:
-            vec[10] = 1.0 / got
-            swap(vec.at[10], x_peers, px.at[1], vec_send.at[10], px_recv.at[1], FAR_X)
-            landed(px.at[1], px_recv.at[1])
+            landed(rb, rc_recv.at[sweep])
+            for k in range(NX):
+                got = vec[at + 2] if k == 0 else rb[k * NC - 1]
+                for m in range(1, NC):
+                    got += rb[k * NC + m - 1]
+                inverse[k] = 1.0 / got
 
     mass = jnp.zeros((per_x, LANES), f32)
     acc = jnp.zeros((per_x, depth), f32)
     for k in range(NX):
-        by = vec[10] if k == 0 else px[1, k - 1]
+        by = inverse[k]
         weights = []
         for t in range(rt):
             got = tile[:, k * npts + t * LANES : k * npts + (t + 1) * LANES] * by[t : t + 1, :]
@@ -360,11 +368,14 @@
             send_piece(h, j, j - 4 if j < 8 else j + 4, 1 if j < 8 else 2)
 
     send_far(0)
+    for j in NEAR:
+        send_piece(0, j, j, 0)
     code_b[...] = coded(acc[:, width:], row_scale)
     send_far(1)
     for h in range(2):
-        for j in NEAR:
-            send_piece(h, j, j, 0)
+        if h == 1:
+            for j in NEAR:
+                send_piece(h, j, j, 0)
         landed(lands[h].at[7], nz_recv.at[h, 3])
         for j, at, slots in ((4, 1, (5, 6, 7)), (12, 2, (9, 10, 11))):
             far = (core == (1 if j == 4 else 0)).astype(f32)
@@ -422,14 +433,14 @@
         h, j = LANDING[n]
         rows = rows_of(h, j)
         landed(rows, agz_recv.at[h, j])
-        if j == 4:
-            on_core(0, lambda: hand_on(rows, agz_recv.at[h, 8], z_peers[3]))
-            for a in (3, 2, 1):
-                hand_on(rows, agz_recv.at[h, 4 + a], z_peers[a - 1])
-        if j == 12:
-            on_core(1, lambda: hand_on(rows, agz_recv.at[h, 8], z_peers[NZ - 5]))
-            for a in (3, 2, 1):
-                hand_on(rows, agz_recv.at[h, 12 - a], z_peers[NZ - a - 1])
+        for at, way, which in ((4, 1, None), (12, -1, None), (6, 1, 0), (10, -1, 1)):
+            if j == at:
+                go = functools.partial(hand_on, rows, agz_recv.at[h, j + 2 * way], z_peers[(2 * way) % NZ - 1])
+                if which is None:
+                    go()
+                else:
+                    on_core(which, go)
+                hand_on(rows, agz_recv.at[h, j + way], z_peers[way % NZ - 1])
         hand_x(n)
         if LAG <= n < LAG + RINGED:
             relay_x(n - LAG)
@@ -469,17 +480,19 @@
             pltpu.VMEM((rt, LANES), f32),
             pltpu.VMEM((rt, LANES), f32),
             pltpu.VMEM((per_x, LANES), f32),
-            pltpu.VMEM((11, ct, LANES), f32),
+            pltpu.VMEM((10, ct, LANES), f32),
             pltpu.VMEM((3, NX - 1, ct, LANES), f32),
             pltpu.VMEM((3, NZ - 1, ct, LANES), f32),
-            pltpu.VMEM((3, NC - 1, rt, LANES), f32),
-            pltpu.VMEM((2, NX - 1, rt, LANES), f32),
+            pltpu.VMEM((2, NC - 1, rt, LANES), f32),
+            pltpu.VMEM((NX * NC - 1, rt, LANES), f32),
+            pltpu.VMEM((NX - 1, rt, LANES), f32),
+            pltpu.VMEM((NX, rt, LANES), f32),
             pltpu.VMEM((per_x, depth // 2 + LANES), bf16),
             pltpu.VMEM((per_x, depth // 2), bf16),
             pltpu.VMEM((NZ - 1, per, depth // 2 + LANES), bf16),
             pltpu.VMEM((NZ - 1, per, depth // 2), bf16),
             dma((5,)), dma, dma((NX - 1,)), dma, dma,
-            dma((11,)), dma((3,)), dma((3,)), dma((3,)), dma((2,)),
+            dma((10,)), dma((3,)), dma((3,)), dma((3,)), dma,
             dma((2,)), dma((2, 4)), dma, dma((2, NZ)), dma, dma((2 * NZ,)),
         ],
         compiler_params=pltpu.CompilerParams(

time: 103 us -> 101 us (0.981); the launches traced: 102 us -> 101 us
  no operation moved by 1% of the time
where the time goes in v7:
time: 101 us
  Pallas kernels  100 us (99%)
  local copies, waits for them, and re-layouts  1.15 us (1%)
    pallas_call x1, Pallas kernels, shards(): pl.pallas_call(functools.partial(kernel, math.log(n_total / k_total), 1.0...  100 us

profile of v7, /device:TPU:6, one launch (start us, length us, event | category | flops | bytes accessed | tf_op | source)
XLA Modules:
  0.0 101.2 jit_solution(17957038796732480157)
XLA Ops:
  0.0 100.1 %balance.1 = bf16[1024,768]{1,0:T(8,128)(2,1)S(1)} custom-call(bf16[1024,768]{1,0:T(8,128)(2,1)} %p_hbm.1, bf16[1024,768]{1,0:T(8,128)(2,1)} %c_hbm.1), custom_call_target="tpu_custom_call" | custom-call | flops 4831838208 | bytes 4718592 | tf_op jit(solution)/shard_map/balance/pallas_call | solution.py:464
  100.1 1.1 %copy.4 = bf16[1024,768]{1,0:T(8,128)(2,1)} copy(bf16[1024,768]{1,0:T(8,128)(2,1)S(1)} %balance.1) | data formatting | bytes 3145728
